TPU v7x, 256 devices: a whole 4x4x8 slice. The times are simulated.
256 devices in a mesh: pert: 64 (over z_hi, x, y), gz: 4 (over z_lo, core).
Axes of the slice: x: 4, y: 4, z: 8 (z_hi: 4, z_lo: 2; z = z_hi * 2 + z_lo), core: 2. Of those that a mesh axis runs over, the one named last changes fastest.
Arguments:
- base_store: float32 [64, 4, 64, 1024], P('pert', None, 'gz'), may hold values from -6 to 6
- perturbations: float32 [128, 4, 64, 1024], P('pert', None, 'gz'), may hold values from -6 to 6
- owner_steps: int32 [3], replicated, may hold values from 0 to 63
- w_in: bfloat16 [64, 108], replicated, may hold values from -0.625 to 0.625
- b_in: float32 [64], replicated, may hold values from -4 to 4
- w_mid: bfloat16 [64, 64], replicated, may hold values from -0.75 to 0.75
- b_mid: float32 [64], replicated, may hold values from -4 to 4
- w_out: bfloat16 [6, 64], replicated, may hold values from -2 to 2
Outputs:
- evolved: float32 [128, 4, 64, 1024], P('pert', None, 'gz')
Inputs may be any that keep to these rules, and one draw needn't show every extreme that they name: `owner_steps`: index along pert of the device that stores each step's base state.
All inputs are finite; a program needn't handle non-finite values.
Results may differ from a plain program's by a relative error of at most 0.0033.
Values sent between devices are 32-bit elements; how exact they have to be, the bound alone decides.
No kernel may reach another device: no remote copies, remote signals or barrier semaphores. Data moves between devices by JAX's collectives and lax.ppermute only.
A program may use at most 64 MiB of HBM per device.

v0:
```python
import jax
import jax.numpy as jnp
from jax import lax
from jax.sharding import PartitionSpec as P

NH = 32
STEPS = 3


TIME_STEP = 0.2


def from_root(shard, axis, root):
    mine = lax.axis_index(axis) == root
    return lax.psum(jnp.where(mine, shard, jnp.zeros_like(shard)), axis)


def with_halo(shard, sides, width):
    for axis, dim in sides:
        size, length = (lax.axis_size(axis), shard.shape[dim])
        up = [(i, (i + 1) % size) for i in range(size - 1)]
        down = [(j, i) for i, j in up]
        last = lax.slice_in_dim(shard, length - width, length, axis=dim)
        leading = lax.slice_in_dim(shard, 0, width, axis=dim)
        before = lax.ppermute(last, axis, up)
        after = lax.ppermute(leading, axis, down)
        shard = jnp.concatenate([before, shard, after], axis=dim)
    return shard


def along_x(field, offset):
    if offset == 0:
        return field
    return jnp.roll(field, -offset * NH, axis=-1)


def along_y(field, offset):
    if offset == 0:
        return field
    plain = jnp.roll(field, -offset, axis=-1)
    wrapped = jnp.roll(field, offset * NH - offset, axis=-1)
    column = jnp.arange(field.shape[-1], dtype=jnp.int32) % NH
    edge = column == (NH - 1 if offset > 0 else 0)
    return jnp.where(edge, wrapped, plain)


def patch_of(slab):
    pieces = []
    for zed in range(3):
        layer_slab = slab[..., zed, :]
        for xed in range(3):
            for yed in range(3):
                pieces.append(along_x(along_y(layer_slab, yed - 1), xed - 1))
    stacked = jnp.stack(pieces, axis=-3)
    return stacked.reshape(stacked.shape[:-3] + (108, stacked.shape[-1]))


def stress_plane(base_pad, pert_pad, center, w_in, b_in, w_mid, b_mid, w_out):
    base_slab = lax.dynamic_slice_in_dim(base_pad, center - 1, 3, axis=1).astype(jnp.bfloat16)
    base_patch = patch_of(base_slab)
    pert_slab = lax.dynamic_slice_in_dim(pert_pad, center - 1, 3, axis=2).astype(jnp.bfloat16)
    pert_patch = patch_of(pert_slab)
    first = jnp.tanh(jnp.dot(w_in, base_patch, preferred_element_type=jnp.float32) + b_in[:, None])
    second = jnp.tanh(
        jnp.dot(w_mid, first.astype(jnp.bfloat16), preferred_element_type=jnp.float32)
        + b_mid[:, None]
    )
    slope_first = 1.0 - first * first
    slope_second = 1.0 - second * second
    lin_one = jnp.einsum("hk,pkc->phc", w_in, pert_patch, preferred_element_type=jnp.float32)
    lift_one = (slope_first * lin_one).astype(jnp.bfloat16)
    lin_two = jnp.einsum("hk,pkc->phc", w_mid, lift_one, preferred_element_type=jnp.float32)
    lift_two = (slope_second * lin_two).astype(jnp.bfloat16)
    return jnp.einsum("hk,pkc->phc", w_out, lift_two, preferred_element_type=jnp.float32)


def advect(base_one, pert_one):
    total = None
    for direction in range(3):
        flux = base_one[direction] * pert_one + pert_one[:, direction : direction + 1] * base_one
        if direction == 0:
            inner = flux[:, :, 1:-1]
            change = along_x(inner, 1) - along_x(inner, -1)
        elif direction == 1:
            inner = flux[:, :, 1:-1]
            change = along_y(inner, 1) - along_y(inner, -1)
        else:
            change = flux[:, :, 2:] - flux[:, :, :-2]
        total = change if total is None else total + change
    return -total


def closure(stress_pad):
    inner = stress_pad[:, :, 1:-1]

    def diff_x(comp):
        return along_x(inner[:, comp], 1) - along_x(inner[:, comp], -1)

    def diff_y(comp):
        return along_y(inner[:, comp], 1) - along_y(inner[:, comp], -1)

    def diff_z(comp):
        return stress_pad[:, comp, 2:] - stress_pad[:, comp, :-2]

    first_row = diff_x(0) + diff_y(3) + diff_z(4)
    second_row = diff_x(3) + diff_y(1) + diff_z(5)
    third_row = diff_x(4) + diff_y(5) + diff_z(2)
    return jnp.stack([first_row, second_row, third_row, jnp.zeros_like(first_row)], axis=1)


def local(base_store, perturbations, owner_steps, w_in, b_in, w_mid, b_mid, w_out):
    plane_count = perturbations.shape[2]
    slab_count = lax.axis_size("gz")
    position = lax.axis_index("gz")
    margin = 2
    state = perturbations
    for step_index in range(STEPS):
        owner_now = owner_steps[step_index]
        owned_slab = from_root(base_store, "pert", owner_now)
        base_pad = with_halo(owned_slab, (("gz", 2),), margin)[0]
        pert_pad = with_halo(state, (("gz", 2),), margin)

        def one_plane(center):
            return stress_plane(base_pad, pert_pad, center, w_in, b_in, w_mid, b_mid, w_out)

        centers = jnp.arange(1, plane_count + 3, dtype=jnp.int32)
        stress_pad = jnp.transpose(lax.map(one_plane, centers), (1, 2, 0, 3))
        levels = position * plane_count + jnp.arange(plane_count + 2, dtype=jnp.int32) - 1
        inside = (levels >= 0) & (levels < slab_count * plane_count)
        stress_pad = jnp.where(inside[:, None], stress_pad, 0.0)
        base_one = base_pad[:, margin - 1 : margin + 1 + plane_count]
        pert_one = pert_pad[:, :, margin - 1 : margin + 1 + plane_count]
        state = state + TIME_STEP * (advect(base_one, pert_one) + closure(stress_pad))
    return state


def solution(mesh):
    in_specs = (
        P("pert", None, "gz", None),
        P("pert", None, "gz", None),
        P(),
        P(),
        P(),
        P(),
        P(),
        P(),
    )
    out_specs = P("pert", None, "gz", None)
    return jax.shard_map(local, mesh=mesh, in_specs=in_specs, out_specs=out_specs, check_vma=False)
```

profile of v0, /device:TPU:1, one launch (start us, length us, event | category | flops | bytes accessed | tf_op | source)
XLA Modules:
  0.0 1991.5 jit_solution(15113130857845078181)
XLA Ops:
  11.8 4.9 collective-permute-start.2
  16.8 1.9 collective-permute-start.3
  24.6 659.4 %all-reduce.3.cloned.1.call-done = (f32[1,4,16,1024]{3,2,1,0:T(8,128)}, f32[1,4,16,1024]{3,2,1,0:T(8,128)}, f32[1,4,16,1024]{3,2,1,0:T(8,128)}) async-done(((f32[1,4,16,1024]{3,2,1,0:T(8,128)}, f32[1,4,16,1024]{3,2,1,0:T(8,128)}, f32[1,4,16,1024]{3,2,1,0:T(8,128)}), (f32[1,4,16,1024]{3,2,1,0:T(8,128)}, f32[1,4,16,1024]{3,2,1,0:T(8,128)}, f32[1,4,16,1024]{3,2,1,0:T(8,128)})) %all-reduce.3.cloned.1.call-update) | async-done | bytes 786448 | tf_op jit(solution)/shard_map/psum | solution.py:15
  684.9 40.3 %collective-permute-start = (f32[1,4,2,1024]{3,2,1,0:T(2,128)S(1)}, f32[1,4,2,1024]{3,2,1,0:T(2,128)S(1)}, u32[]{:S(2)}, u32[]{:S(2)}) collective-permute-start(f32[1,4,2,1024]{3,2,1,0:T(2,128)S(1)} %get-tuple-element.1505), channel_id=1, source_target_pairs={{0,1},{1,2},{2,3},{4,5},{5,6},{6,7},{8,9},{9,10},{10,11},{12,13},{... | collective-permute-start | bytes 98312 | tf_op jit(solution)/shard_map/ppermute | solution.py:25
  725.2 1.9 collective-permute-start.1
  728.8 3.6 collective-permute-start.4
  732.4 1.9 collective-permute-start.5
  736.0 3.6 collective-permute-start.8
  739.7 2.1 collective-permute-start.9
  743.5 483.4 %while.42 = (s32[]{:T(128)}, f32[18,2,6,1024]{3,0,1,2:T(8,128)S(1)}, s32[18]{0:T(128)}, bf16[4,20,1024]{2,0,1:T(4,128)(2,1)S(1)}, bf16[64,108]{1,0:T(8,128)(2,1)...) while((s32[]{:T(128)}, ...), condition=%wide.region_2.3_spmd, body=%wide.region_1.2_spmd.sunk | while | flops 72415232 | bytes 7833315 | solution.py:127
  1236.6 3.6 collective-permute-start.6
  1240.3 2.1 collective-permute-start.7
  1243.3 2.6 collective-permute-done.7
  1248.4 391.2 %while.43 = (s32[]{:T(128)}, f32[18,2,6,1024]{3,0,1,2:T(8,128)}, s32[18]{0:T(128)}, bf16[4,20,1024]{2,0,1:T(4,128)(2,1)}, bf16[64,108]{1,0:T(8,128)(2,1)S(1)}, /...) while((s32[]{:T(128)}, f32[18,2,6,1024]{3,0,1,2:T(8,128)}, ...), condition=%wide.region_5.6_spmd, body=%wide.region_4.5_spmd.sunk | while | flops 72415232 | bytes 7842507 | solution.py:127
  1442.1 1.9 dynamic_update_slice.32
  1463.8 1.9 dynamic_update_slice.32
  1485.6 1.9 dynamic_update_slice.32
  1507.3 1.9 dynamic_update_slice.32
  1529.0 1.9 dynamic_update_slice.32
  1550.8 1.9 dynamic_update_slice.32
  1572.5 1.9 dynamic_update_slice.32
  1594.2 1.9 dynamic_update_slice.32
  1646.2 1.9 collective-permute-start.10
  1648.1 2.6 collective-permute-start.11
  1655.5 322.1 %while.44 = (s32[]{:T(128)}, f32[18,2,6,1024]{3,0,1,2:T(8,128)}, s32[18]{0:T(128)}, bf16[4,20,1024]{2,0,1:T(4,128)(2,1)}, bf16[64,108]{1,0:T(8,128)(2,1)S(1)}, /...) while((s32[]{:T(128)}, f32[18,2,6,1024]{3,0,1,2:T(8,128)}, ...), condition=%wide.region_8.9_spmd, body=%wide.region_7.8_spmd.sunk | while | flops 72415232 | bytes 7845611 | solution.py:127
  1814.7 1.9 dynamic_update_slice.33
  1832.6 1.9 dynamic_update_slice.33
  1850.5 1.9 dynamic_update_slice.33
  1868.4 1.9 dynamic_update_slice.33
  1886.3 1.9 dynamic_update_slice.33
  1904.2 1.9 dynamic_update_slice.33
  1922.1 1.9 dynamic_update_slice.33
  (7433 shorter events, 1136.3 us)
Async XLA Ops:
  6.5 677.4 %all-reduce.3.cloned.1.call-start = ((), (), s32[]{:S(2)}) async-start(), calls=%async_computation | async-start | bytes 1572864 | tf_op jit(solution)/shard_map/psum | solution.py:15
  11.8 9.2 collective-permute-start.2
  16.8 5.6 collective-permute-start.3
  684.9 54.7 %collective-permute-start = (f32[1,4,2,1024]{3,2,1,0:T(2,128)S(1)}, f32[1,4,2,1024]{3,2,1,0:T(2,128)S(1)}, u32[]{:S(2)}, u32[]{:S(2)}) collective-permute-start(f32[1,4,2,1024]{3,2,1,0:T(2,128)S(1)} %get-tuple-element.1505), channel_id=1, source_target_pairs={{0,1},{1,2},{2,3},{4,5},{5,6},{6,7},{8,9},{9,10},{10,11},{12,13},{... | collective-permute-start | bytes 98312 | tf_op jit(solution)/shard_map/ppermute | solution.py:25
  725.2 16.5 collective-permute-start.1
  728.8 505.1 %collective-permute-start.4 = (f32[1,4,2,1024]{3,2,1,0:T(2,128)}, f32[1,4,2,1024]{3,2,1,0:T(2,128)}, u32[]{:S(2)}, u32[]{:S(2)}) collective-permute-start(f32[1,4,2,1024]{3,2,1,0:T(2,128)} %get-tuple-element.1503), channel_id=1, source_target_pairs={{0,1},{1,2},{2,3},{4,5},{5,6},{6,7},{8,9},{9,10},{10,11},{12,13},{... | collective-permute-start | bytes 98312 | tf_op jit(solution)/shard_map/ppermute | solution.py:25
  732.4 501.5 %collective-permute-start.5 = (f32[1,4,2,1024]{3,2,1,0:T(2,128)}, f32[1,4,2,1024]{3,2,1,0:T(2,128)}, u32[]{:S(2)}, u32[]{:S(2)}) collective-permute-start(f32[1,4,2,1024]{3,2,1,0:T(2,128)} %get-tuple-element.1504), channel_id=1, source_target_pairs={{1,0},{2,1},{3,2},{5,4},{6,5},{7,6},{9,8},{10,9},{11,10},{13,12},{... | collective-permute-start | bytes 98312 | tf_op jit(solution)/shard_map/ppermute | solution.py:26
  736.0 506.4 %collective-permute-start.8 = (f32[1,4,2,1024]{3,2,1,0:T(2,128)}, f32[1,4,2,1024]{3,2,1,0:T(2,128)}, u32[]{:S(2)}, u32[]{:S(2)}) collective-permute-start(f32[1,4,2,1024]{3,2,1,0:T(2,128)} %get-tuple-element.1501), channel_id=1, source_target_pairs={{0,1},{1,2},{2,3},{4,5},{5,6},{6,7},{8,9},{9,10},{10,11},{12,13},{... | collective-permute-start | bytes 98312 | tf_op jit(solution)/shard_map/ppermute | solution.py:25
  739.7 502.7 %collective-permute-start.9 = (f32[1,4,2,1024]{3,2,1,0:T(2,128)}, f32[1,4,2,1024]{3,2,1,0:T(2,128)}, u32[]{:S(2)}, u32[]{:S(2)}) collective-permute-start(f32[1,4,2,1024]{3,2,1,0:T(2,128)} %get-tuple-element.1502), channel_id=1, source_target_pairs={{1,0},{2,1},{3,2},{5,4},{6,5},{7,6},{9,8},{10,9},{11,10},{13,12},{... | collective-permute-start | bytes 98312 | tf_op jit(solution)/shard_map/ppermute | solution.py:26
  757.8 11.0 copy-start.19
  784.7 11.0 copy-start.19
  811.6 11.0 copy-start.19
  838.4 11.0 copy-start.19
  865.3 11.0 copy-start.19
  892.1 11.0 copy-start.19
  919.0 11.0 copy-start.19
  945.8 11.0 copy-start.19
  972.7 11.0 copy-start.19
  999.5 11.0 copy-start.19
  1026.4 11.0 copy-start.19
  1053.2 11.0 copy-start.19
  1080.1 11.0 copy-start.19
  1107.0 11.0 copy-start.19
  1133.8 11.0 copy-start.19
  1160.7 11.0 copy-start.19
  1187.5 11.0 copy-start.19
  1214.4 11.0 copy-start.19
  1236.6 6.6 collective-permute-start.6
  1240.3 5.6 collective-permute-start.7
  1646.2 6.2 collective-permute-start.10
  1648.1 5.6 collective-permute-start.11
  1655.5 322.1 %copy-start.25 = (pred[18]{0:T(512)(128)(4,1)S(1)}, pred[18]{0:T(512)(128)(4,1)}, u32[]{:S(2)}) copy-start(pred[18]{0:T(512)(128)(4,1)} %compare_and_fusion) | copy-start | bytes 58
  (43 other events, 88.3 us)
Sparse Core Ops, SparseCore 0:
  11.9 672.0 all-reduce.2
where the time goes:
time: 2010 us; the launch traced here: 1990 us
  waiting for transfers between devices  665 us (33%)
  local copies, waits for them, and re-layouts  651 us (32%)
  other arithmetic  392 us (20%)
  matrix products  119 us (6%)
  loops' own time  77.8 us (4%)
  starting transfers between devices  70.6 us (4%)
    psum x1, waiting for transfers between devices, from_root(): return lax.psum(jnp.where(mine, shard, jnp.zeros_like(shard)), axis)  659 us
    while x2484, other arithmetic  340 us
    slice x1734, local copies, waits for them, and re-layouts, along_x(): return jnp.roll(field, -offset * NH, axis=-1)  166 us
    concatenate x666, local copies, waits for them, and re-layouts, along_y(): plain = jnp.roll(field, -offset, axis=-1)  98.5 us
    dynamic_update_slice x108, local copies, waits for them, and re-layouts, local(): stress_pad = jnp.transpose(lax.map(one_plane, centers), (1, 2, 0, 3))  80.7 us
    another operation x3, loops' own time, local(): stress_pad = jnp.transpose(lax.map(one_plane, centers), (1, 2, 0, 3))  77.8 us
    slice x438, local copies, waits for them, and re-layouts, along_y(): plain = jnp.roll(field, -offset, axis=-1)  76.3 us
    concatenate x450, local copies, waits for them, and re-layouts, along_y(): wrapped = jnp.roll(field, offset * NH - offset, axis=-1)  69.7 us

commit v1 on v0

v1 whole, which is shorter than its diff:
```python
import functools

import jax
import jax.numpy as jnp
from jax import lax
from jax.experimental import pallas as pl
from jax.experimental.pallas import tpu as pltpu
from jax.sharding import Mesh, PartitionSpec as P

NH = 32
STEPS = 3
TIME_STEP = 0.2
PLANES = 16
HALO = 6
EXT = PLANES + 2 * HALO
BLOCK = 8
SHIFT = BLOCK - HALO
PLANE = 1024
UNITS = 64
LANES = 128
CHUNK = 256
PROWS = 80
BROWS = 48


def shift_y(v, column):
    up = jnp.where(column == NH - 1, pltpu.roll(v, NH - 1, 1), pltpu.roll(v, LANES - 1, 1))
    down = jnp.where(column == 0, pltpu.roll(v, LANES - NH + 1, 1), pltpu.roll(v, 1, 1))
    return down, up


def shift_x(parts, lane):
    n = len(parts)
    left = [pltpu.roll(v, LANES - NH, 1) for v in parts]
    right = [pltpu.roll(v, NH, 1) for v in parts]
    up = [jnp.where(lane < LANES - NH, left[k], left[(k + 1) % n]) for k in range(n)]
    down = [jnp.where(lane >= NH, right[k], right[(k - 1) % n]) for k in range(n)]
    return down, up


def kernel(place, own, low, high, r0, r1, r2, r3, wp, wb, wm, wm2, wo, b_in, b_mid, out,
           st, base, pp, bp, part, gz, bias):
    f32, bf16 = jnp.float32, jnp.bfloat16
    lane = lax.broadcasted_iota(jnp.int32, (8, LANES), 1)
    column = lane % NH
    upper = lax.broadcasted_iota(jnp.int32, (8, LANES), 0) < 4
    upper_wide = lax.broadcasted_iota(jnp.int32, (8, CHUNK), 0) < 4
    parts = PLANE // LANES
    y_now, slab, slabs = place[0], place[1], place[2]

    st[0:HALO] = low[...]
    st[HALO : HALO + PLANES] = own[...]
    st[HALO + PLANES :] = high[...]
    bias[0] = jnp.broadcast_to(b_in[...], (UNITS, CHUNK))
    bias[1] = jnp.broadcast_to(b_mid[...], (UNITS, CHUNK))
    pad = jnp.zeros((8, LANES), f32)

    def inside(e):
        level = slab * PLANES + e - HALO
        return jnp.logical_and(level >= 0, level < slabs * PLANES)

    for step in range(STEPS):
        lo, hi = 2 * step, EXT - 2 * step

        for k, ref in enumerate((r0, r1, r2, r3)):
            start = lax.rem(y_now + 4 - k, 4) * BLOCK

            @pl.loop(0, BLOCK)
            def _(z):
                rows = ref[step, z]
                base[start + z, 0:4] = rows
                base[start + z, 4:8] = rows

        @pl.loop(lo, hi)
        def _(e):
            mid = [st[e, :, k * LANES : (k + 1) * LANES] for k in range(parts)]
            moved = [shift_y(v, column) for v in mid]
            rows = []
            thirds = [[m[0] for m in moved], mid, [m[1] for m in moved]]
            moved_x = [shift_x(third, lane) for third in thirds]
            for xed in range(3):
                for yed in range(3):
                    rows.append(thirds[yed] if xed == 1 else moved_x[yed][xed // 2])
            for t in range(5):
                for k in range(parts):
                    second = rows[2 * t + 1][k] if 2 * t + 1 < 9 else pad
                    pair = jnp.concatenate([rows[2 * t][k], second], axis=0)
                    pp[e, 16 * t : 16 * t + 16, k * LANES : (k + 1) * LANES] = pair.astype(bf16)
            mid = [base[e + SHIFT, :, k * LANES : (k + 1) * LANES] for k in range(parts)]
            both = []
            for v in mid:
                down, up = shift_y(v, column)
                both.append(jnp.where(upper, down, up))
            both_down, both_up = shift_x(both, lane)
            mid_down, mid_up = shift_x(mid, lane)
            sides = [jnp.where(upper, a, b) for a, b in zip(mid_down, mid_up)]
            rows = [both_down, both, both_up, sides, mid, [pad] * parts]
            for t in range(3):
                for k in range(parts):
                    pair = jnp.concatenate([rows[2 * t][k], rows[2 * t + 1][k]], axis=0)
                    bp[e, 16 * t : 16 * t + 16, k * LANES : (k + 1) * LANES] = pair.astype(bf16)

        @pl.loop(lo + 1, hi - 1)
        def _(e):
            keep = inside(e)
            gx, gy = [], []
            for n in range(PLANE // CHUNK):
                cells = slice(n * CHUNK, (n + 1) * CHUNK)
                patch = pp[pl.ds(e - 1, 3), :, cells].reshape(3 * PROWS, CHUNK)
                base_patch = bp[pl.ds(e - 1, 3), :, cells].reshape(3 * BROWS, CHUNK)
                first = jnp.tanh(jnp.dot(wb[...], base_patch, preferred_element_type=f32) + bias[0])
                second = jnp.tanh(
                    jnp.dot(wm[...], first.astype(bf16), preferred_element_type=f32) + bias[1]
                )
                slope_first = 1.0 - first * first
                slope_second = 1.0 - second * second
                lin_one = jnp.dot(wp[...], patch, preferred_element_type=f32)
                lift_one = jnp.concatenate(
                    [slope_first * lin_one[:UNITS], slope_first * lin_one[UNITS:]], axis=0
                ).astype(bf16)
                lin_two = jnp.dot(wm2[...], lift_one, preferred_element_type=f32)
                lift_two = jnp.concatenate(
                    [slope_second * lin_two[:UNITS], slope_second * lin_two[UNITS:]], axis=0
                ).astype(bf16)
                stress = jnp.dot(wo[...], lift_two, preferred_element_type=f32)
                stress = jnp.where(keep, stress, 0.0)
                v = st[e, :, cells]
                u = base[e + SHIFT, :, cells]
                g = []
                for j in range(3):
                    u_j = base[e + SHIFT, j : j + 1, cells]
                    v_j = jnp.where(upper_wide, st[e, j : j + 1, cells], st[e, 4 + j : 5 + j, cells])
                    g.append(stress[8 * j : 8 * j + 8] - (u_j * v + v_j * u))
                gz[e, :, cells] = g[2]
                for half in range(CHUNK // LANES):
                    gx.append(g[0][:, half * LANES : (half + 1) * LANES])
                    gy.append(g[1][:, half * LANES : (half + 1) * LANES])
            down_x, up_x = shift_x(gx, lane)
            for k in range(parts):
                down_y, up_y = shift_y(gy[k], column)
                part[e, :, k * LANES : (k + 1) * LANES] = (up_x[k] - down_x[k]) + (up_y - down_y)

        @pl.loop(lo + 2, hi - 2)
        def _(e):
            new = st[e] + TIME_STEP * (part[e] + (gz[e + 1] - gz[e - 1]))
            if step == STEPS - 1:
                out[e - HALO] = new
            else:
                st[e] = jnp.where(inside(e), new, 0.0)


def weights_of(w_in, w_mid, w_out):
    bf16 = jnp.bfloat16
    eye = jnp.eye(2, dtype=bf16)
    split = jnp.pad(w_in.reshape(UNITS, 3, 9, 4), ((0, 0), (0, 0), (0, 1), (0, 0)))
    wp = eye[:, None, None, None, :, None] * split[None, :, :, :, None, :]
    wp = wp.reshape(2 * UNITS, 3 * PROWS)
    order = (0, 2, 3, 5, 6, 8, 1, 7, 4, 9, 9, 9)
    wb = jnp.concatenate([split[:, :, i : i + 1] for i in order], axis=2).reshape(UNITS, 3 * BROWS)
    wm2 = (eye[:, None, :, None] * w_mid[None, :, None, :]).reshape(2 * UNITS, 2 * UNITS)
    out_pad = jnp.pad(w_out, ((0, 1), (0, 0)))
    comps = (0, 3, 4, 6, 3, 1, 5, 6, 4, 5, 2, 6)
    rows = jnp.concatenate([out_pad[i : i + 1] for i in comps], axis=0).reshape(3, 1, 4, 1, UNITS)
    wo = (rows * eye[None, :, None, :, None]).reshape(24, 2 * UNITS)
    return wp, wb, w_mid, wm2, wo


def pick(options, which):
    chosen = options[0]
    for k in range(1, len(options)):
        chosen = jnp.where(which == k, options[k], chosen)
    return chosen


def around(piece, axis):
    return [piece] + [
        lax.ppermute(piece, axis, [(i, (i + k) % 4) for i in range(4)]) for k in (1, 2, 3)
    ]


def spread_base(base_store, owner_steps, slabs):
    x, y, h = (lax.axis_index(a) for a in ("x", "y", "h"))
    owner_h, owner_x, owner_y = (owner_steps // 16, (owner_steps // 4) % 4, owner_steps % 4)
    blocks = jnp.transpose(base_store[0].reshape(4, 2, BLOCK, PLANE), (1, 2, 0, 3))
    come = []
    for k in range(4):
        pairs = []
        for target in range(4):
            source = (target - k) % 4
            for slab in range(slabs):
                other = slab + (-1, 0, 0, 1)[target]
                if 0 <= other < slabs:
                    pairs.append((source * slabs + other, target * slabs + slab))
        target = (y + k) % 4
        send = jnp.where(target % 2 == 0, blocks[1], blocks[0])
        come.append(lax.ppermute(send, ("y", "gz"), pairs))
    mine = jnp.stack([pick(come, (y - owner_y[s]) % 4) for s in range(STEPS)])
    width = PLANE // 4

    def cells_of(which):
        return lax.dynamic_slice_in_dim(mine, which * width, width, axis=3)

    come = [cells_of(x)]
    for k in (1, 2, 3):
        pairs = [(i, (i + k) % 4) for i in range(4)]
        come.append(lax.ppermute(cells_of((x + k) % 4), "x", pairs))
    mine = jnp.stack([pick([c[s] for c in come], (x - owner_x[s]) % 4) for s in range(STEPS)])
    come = around(mine, "h")
    mine = jnp.stack([pick([c[s] for c in come], (h - owner_h[s]) % 4) for s in range(STEPS)])
    come = around(mine, "x")
    ring = [come[0], come[3], come[2], come[1]]
    whole = jnp.concatenate([pick([ring[(j - i) % 4] for i in range(4)], x) for j in range(4)], axis=3)
    return around(whole, "y")


def local(base_store, perturbations, owner_steps, w_in, b_in, w_mid, b_mid, w_out):
    slabs = lax.axis_size("gz")
    slab = lax.axis_index("gz")
    state = jnp.transpose(perturbations.reshape(8, PLANES, PLANE), (1, 0, 2))
    up = [(i, i + 1) for i in range(slabs - 1)]
    down = [(j, i) for i, j in up]
    low = lax.ppermute(state[PLANES - HALO :], "gz", up)
    high = lax.ppermute(state[:HALO], "gz", down)
    come = spread_base(base_store, owner_steps, slabs)
    place = jnp.stack([lax.axis_index("y"), slab, jnp.int32(slabs)]).astype(jnp.int32)
    vmem = pl.BlockSpec(memory_space=pltpu.VMEM)
    f32, bf16 = jnp.float32, jnp.bfloat16
    new = pl.pallas_call(
        kernel,
        out_shape=jax.ShapeDtypeStruct((PLANES, 8, PLANE), f32),
        in_specs=[pl.BlockSpec(memory_space=pltpu.SMEM)] + [vmem] * 14,
        out_specs=vmem,
        scratch_shapes=[
            pltpu.VMEM((EXT, 8, PLANE), f32),
            pltpu.VMEM((4 * BLOCK, 8, PLANE), f32),
            pltpu.VMEM((EXT, PROWS, PLANE), bf16),
            pltpu.VMEM((EXT, BROWS, PLANE), bf16),
            pltpu.VMEM((EXT, 8, PLANE), f32),
            pltpu.VMEM((EXT, 8, PLANE), f32),
            pltpu.VMEM((2, UNITS, CHUNK), f32),
        ],
        compiler_params=pltpu.CompilerParams(vmem_limit_bytes=40 * 2**20),
    )(place, state, low, high, *come, *weights_of(w_in, w_mid, w_out), b_in[:, None], b_mid[:, None])
    return jnp.transpose(new, (1, 0, 2)).reshape(perturbations.shape)


def solution(mesh):
    spec = P(("h", "x", "y"), None, "gz", None)
    fine = Mesh(mesh.devices.reshape(4, 4, 4, mesh.devices.shape[1]), ("h", "x", "y", "gz"))
    in_specs = (spec, spec, P(), P(), P(), P(), P(), P())
    return jax.shard_map(local, mesh=fine, in_specs=in_specs, out_specs=spec, check_vma=False)
```

time: 2010 us -> 202 us (0.10)
  local copies, waits for them, and re-layouts: 651 us -> 8.29 us
  waiting for transfers between devices: 665 us -> 25.7 us
  other arithmetic: 392 us -> 1.17 us
  matrix products: 119 us -> 0 us
  Pallas kernels: 0 us -> 118 us
  loops' own time: 77.8 us -> 0 us
  starting transfers between devices: 70.6 us -> 41.3 us
    psum x1 -> x0, waiting for transfers between devices: 659 us -> none  [from_root(): return lax.psum(jnp.where(mine, shard, jnp.zeros_like(shard)), axis)]
    while x2484 -> x0, other arithmetic: 340 us -> none
    slice x2188 -> x6, local copies, waits for them, and re-layouts: 249 us -> 1.34 us  [the longest x1 0.65 us: spread_base(): owner_h[s]]
    concatenate x1132 -> x2, local copies, waits for them, and re-layouts: 170 us -> 0.07 us  [the longest x1 0.06 us: weights_of(): jnp.concatenate([out_pad[i:i + 1] for i in comps], axis=0)]
    dot_general x216 -> x0, matrix products: 119 us -> none  [the longest x54 45.1 us: stress_plane(): jnp.dot(w_in, base_patch, preferred_element_type=jnp.float32)]
    pallas_call x0 -> x1, Pallas kernels: none -> 118 us  [local(): pl.pallas_call(kernel, out_shape=jax.ShapeDtypeStruct((PLANES, 8, PLANE),...]
    dynamic_update_slice x108 -> x0, local copies, waits for them, and re-layouts: 80.7 us -> none  [local(): stress_pad = jnp.transpose(lax.map(one_plane, centers), (1, 2, 0, 3))]
    another operation x3 -> x0, loops' own time: 77.8 us -> none  [local(): stress_pad = jnp.transpose(lax.map(one_plane, centers), (1, 2, 0, 3))]
where the time goes in v1:
time: 202 us; the launch traced here: 201 us
  Pallas kernels  118 us (58%)
  starting transfers between devices  41.3 us (20%)
  waiting for transfers between devices  25.7 us (13%)
  local copies, waits for them, and re-layouts  8.29 us (4%)
  between operations  6.28 us (3%)
    pallas_call x1, Pallas kernels, local(): pl.pallas_call(kernel, out_shape=jax.ShapeDtypeStruct((PLANES, 8, PLANE),...  118 us
    ppermute x9, waiting for transfers between devices, around(): lax.ppermute(piece, axis, [(i, (i + k) % 4) for i in range(4)])  22.6 us
    ppermute x9, starting transfers between devices, around(): lax.ppermute(piece, axis, [(i, (i + k) % 4) for i in range(4)])  17.7 us
    ppermute x4, starting transfers between devices, spread_base(): come.append(lax.ppermute(send, ('y', 'gz'), pairs))  13.8 us
    unnamed x25, local copies, waits for them, and re-layouts  4.56 us
    ppermute x3, starting transfers between devices, spread_base(): come.append(lax.ppermute(cells_of((x + k) % 4), 'x', pairs))  4.29 us
  transfers between devices with their start and end apart: 18, of which 8 were waited for; matrix products, arithmetic and copies ran while one was open for 2% of the time, Pallas kernels for 0%

profile of v1, /device:TPU:1, one launch (start us, length us, event | category | flops | bytes accessed | tf_op | source)
XLA Modules:
  0.0 201.1 jit_solution(4583323315984557310)
XLA Ops:
  0.0 1.1 copy.15
  1.3 5.1 %collective-permute-start.5 = (f32[8,4,1024]{2,1,0:T(4,128)S(1)}, f32[8,4,1024]{2,1,0:T(4,128)S(1)}, u32[]{:S(2)}, u32[]{:S(2)}) collective-permute-start(f32[8,4,1024]{2,1,0:T(4,128)S(1)} %get-tuple-element.21), channel_id=1, source_target_pairs={{0,1},{1,2},{2,3},{4,4},{5,5},{6,6},{7,7},{8,8},{9,9},{10,10},{11,... | collective-permute-start | bytes 393224 | tf_op jit(solution)/shard_map/ppermute | solution.py:196
  6.3 1.9 collective-permute-start.4
  8.3 4.9 %collective-permute-start.2 = (f32[8,4,1024]{2,1,0:T(4,128)S(1)}, f32[8,4,1024]{2,1,0:T(4,128)S(1)}, u32[]{:S(2)}, u32[]{:S(2)}) collective-permute-start(f32[8,4,1024]{2,1,0:T(4,128)S(1)} %get-tuple-element.23), channel_id=1, source_target_pairs={{4,1},{5,2},{6,3},{8,4},{9,5},{10,6},{11,7},{12,8},{13,9},{14,10},... | collective-permute-start | bytes 393224 | tf_op jit(solution)/shard_map/ppermute | solution.py:196
  13.1 1.9 collective-permute-start.3
  15.4 1.9 collective-permute-start.1
  17.4 0.6 copy-done.6
  18.1 0.6 fusion.18
  20.7 0.7 copy-done.3
  22.8 3.6 %collective-permute-start = (f32[6,8,1024]{2,1,0:T(8,128)S(1)}, f32[6,8,1024]{2,1,0:T(8,128)S(1)}, u32[]{:S(2)}, u32[]{:S(2)}) collective-permute-start(f32[6,8,1024]{2,1,0:T(8,128)S(1)} %get-tuple-element.11), channel_id=1, source_target_pairs={{0,1},{1,2},{2,3},{4,5},{5,6},{6,7},{8,9},{9,10},{10,11},{12,13},{... | collective-permute-start | bytes 589832 | tf_op jit(solution)/shard_map/ppermute | solution.py:222
  26.8 2.6 %collective-permute-start.6 = (f32[3,8,4,256]{3,2,1,0:T(4,128)S(1)}, f32[3,8,4,256]{3,2,1,0:T(4,128)S(1)}, u32[]{:S(2)}, u32[]{:S(2)}) collective-permute-start(f32[3,8,4,256]{3,2,1,0:T(4,128)S(1)} %get-tuple-element.16), channel_id=1, source_target_pairs={{0,48},{16,0},{32,16},{48,32},{1,49},{17,1},{33,17},{49,33},{2,50}... | collective-permute-start | bytes 294920 | tf_op jit(solution)/shard_map/ppermute | solution.py:206
  29.4 1.7 collective-permute-start.7
  31.1 0.7 fusion.16
  33.7 3.0 %collective-permute-done.8 = f32[3,8,4,256]{3,2,1,0:T(4,128)S(1)} collective-permute-done((f32[3,8,4,256]{3,2,1,0:T(4,128)S(1)}, f32[3,8,4,256]{3,2,1,0:T(4,128)S(1)}, u32[]{:S(2)}, u32[]{:S(2)}) %collective-permute-start.8) | collective-permute-done | bytes 98336 | tf_op jit(solution)/shard_map/ppermute | solution.py:206
  36.8 3.1 %collective-permute-start.11 = (f32[3,8,4,256]{3,2,1,0:T(4,128)S(1)}, f32[3,8,4,256]{3,2,1,0:T(4,128)S(1)}, u32[]{:S(2)}, u32[]{:S(2)}) collective-permute-start(f32[3,8,4,256]{3,2,1,0:T(4,128)S(1)} %pad_maximum_fusion.2), channel_id=1, source_target_pairs={{0,64},{64,128},{128,192},{192,0},{1,65},{65,129},{129,193},{193,1... | collective-permute-start | bytes 294920 | tf_op jit(solution)/shard_map/ppermute | solution.py:177
  39.9 4.6 %collective-permute-start.10 = (f32[3,8,4,256]{3,2,1,0:T(4,128)S(1)}, f32[3,8,4,256]{3,2,1,0:T(4,128)S(1)}, u32[]{:S(2)}, u32[]{:S(2)}) collective-permute-start(f32[3,8,4,256]{3,2,1,0:T(4,128)S(1)} %pad_maximum_fusion.2), channel_id=1, source_target_pairs={{0,128},{64,192},{128,0},{192,64},{1,129},{65,193},{129,1},{193,65... | collective-permute-start | bytes 294920 | tf_op jit(solution)/shard_map/ppermute | solution.py:177
  44.5 2.4 %collective-permute-start.9 = (f32[3,8,4,256]{3,2,1,0:T(4,128)S(1)}, f32[3,8,4,256]{3,2,1,0:T(4,128)S(1)}, u32[]{:S(2)}, u32[]{:S(2)}) collective-permute-start(f32[3,8,4,256]{3,2,1,0:T(4,128)S(1)} %pad_maximum_fusion.2), channel_id=1, source_target_pairs={{0,192},{64,0},{128,64},{192,128},{1,193},{65,1},{129,65},{193,129... | collective-permute-start | bytes 294920 | tf_op jit(solution)/shard_map/ppermute | solution.py:177
  48.9 1.8 collective-permute-done.10
  50.6 1.2 collective-permute-done.9
  52.3 1.8 collective-permute-start.13
  54.1 2.0 collective-permute-start.12
  56.1 0.7 copy-done.4
  56.9 0.7 copy-done.5
  57.6 0.7 collective-permute-done.14
  59.0 1.5 collective-permute-start.17
  60.6 1.2 collective-permute-start.16
  61.8 0.8 collective-permute-start.15
  63.1 4.4 %collective-permute-done.17.r3 = f32[3,8,4,1024]{3,2,1,0:T(4,128)S(1)} collective-permute-done((f32[3,8,4,1024]{3,2,1,0:T(4,128)S(1)}, f32[3,8,4,1024]{3,2,1,0:T(4,128)S(1)}, u32[]{:S(2)}, u32[]{:S(2)}) %collective-permute-start.17) | collective-permute-done | bytes 393248 | tf_op jit(solution)/shard_map/ppermute | solution.py:177
  67.4 3.1 %collective-permute-done.16.r2 = f32[3,8,4,1024]{3,2,1,0:T(4,128)S(1)} collective-permute-done((f32[3,8,4,1024]{3,2,1,0:T(4,128)S(1)}, f32[3,8,4,1024]{3,2,1,0:T(4,128)S(1)}, u32[]{:S(2)}, u32[]{:S(2)}) %collective-permute-start.16) | collective-permute-done | bytes 393248 | tf_op jit(solution)/shard_map/ppermute | solution.py:177
  70.5 11.0 %collective-permute-done.15.r1 = f32[3,8,4,1024]{3,2,1,0:T(4,128)S(1)} collective-permute-done((f32[3,8,4,1024]{3,2,1,0:T(4,128)S(1)}, f32[3,8,4,1024]{3,2,1,0:T(4,128)S(1)}, u32[]{:S(2)}, u32[]{:S(2)}) %collective-permute-start.15) | collective-permute-done | bytes 393248 | tf_op jit(solution)/shard_map/ppermute | solution.py:177
  81.5 118.5 %shard_map.82 = f32[16,8,1024]{2,1,0:T(8,128)S(1)} custom-call(s32[3]{0:T(128)S(1)} %pad_add_fusion.place, f32[16,8,1024]{2,1,0:T(8,128)S(1)} %bitcast.42, f32[6,8,1024]{2,1,0:T(8,128)S(1)} %collective-permute-done.low, f32[6,8,1024]{2,1,0:T(8,128)S(1)} %collective-permute-done.1.high, f32[3,8,4,1024]{3,2,1,0:T(4,128)S(1)} %pad_maximum_fusion.1.r0, ...), custom_call_target="tpu_custom_call" | custom-call | tf_op jit(solution)/shard_map/pallas_call | solution.py:228
  200.0 1.1 copy.25
  (69 shorter events, 4.1 us)
Async XLA Ops:
  1.1 13.9 %copy-start.1 = (f32[2,4,16,1024]{3,2,1,0:T(8,128)S(1)}, f32[2,4,16,1024]{3,2,1,0:T(8,128)}, u32[]{:S(2)}) copy-start(f32[2,4,16,1024]{3,2,1,0:T(8,128)} %param.9) | copy-start | bytes 1572868
  1.3 21.6 %collective-permute-start.5 = (f32[8,4,1024]{2,1,0:T(4,128)S(1)}, f32[8,4,1024]{2,1,0:T(4,128)S(1)}, u32[]{:S(2)}, u32[]{:S(2)}) collective-permute-start(f32[8,4,1024]{2,1,0:T(4,128)S(1)} %get-tuple-element.21), channel_id=1, source_target_pairs={{0,1},{1,2},{2,3},{4,4},{5,5},{6,6},{7,7},{8,8},{9,9},{10,10},{11,... | collective-permute-start | bytes 393224 | tf_op jit(solution)/shard_map/ppermute | solution.py:196
  6.3 20.2 %collective-permute-start.4 = (f32[8,4,1024]{2,1,0:T(4,128)S(1)}, f32[8,4,1024]{2,1,0:T(4,128)S(1)}, u32[]{:S(2)}, u32[]{:S(2)}) collective-permute-start(f32[8,4,1024]{2,1,0:T(4,128)S(1)} %get-tuple-element.22), channel_id=1, source_target_pairs={{12,1},{13,2},{14,3},{0,4},{1,5},{2,6},{3,7},{4,8},{5,9},{6,10},{7... | collective-permute-start | bytes 393224 | tf_op jit(solution)/shard_map/ppermute | solution.py:196
  8.3 18.2 %collective-permute-start.2 = (f32[8,4,1024]{2,1,0:T(4,128)S(1)}, f32[8,4,1024]{2,1,0:T(4,128)S(1)}, u32[]{:S(2)}, u32[]{:S(2)}) collective-permute-start(f32[8,4,1024]{2,1,0:T(4,128)S(1)} %get-tuple-element.23), channel_id=1, source_target_pairs={{4,1},{5,2},{6,3},{8,4},{9,5},{10,6},{11,7},{12,8},{13,9},{14,10},... | collective-permute-start | bytes 393224 | tf_op jit(solution)/shard_map/ppermute | solution.py:196
  13.1 13.4 %collective-permute-start.3 = (f32[8,4,1024]{2,1,0:T(4,128)S(1)}, f32[8,4,1024]{2,1,0:T(4,128)S(1)}, u32[]{:S(2)}, u32[]{:S(2)}) collective-permute-start(f32[8,4,1024]{2,1,0:T(4,128)S(1)} %get-tuple-element.24), channel_id=1, source_target_pairs={{8,1},{9,2},{10,3},{12,4},{13,5},{14,6},{15,7},{0,8},{1,9},{2,10},... | collective-permute-start | bytes 393224 | tf_op jit(solution)/shard_map/ppermute | solution.py:196
  15.4 47.7 %collective-permute-start.1 = (f32[6,8,1024]{2,1,0:T(8,128)S(1)}, f32[6,8,1024]{2,1,0:T(8,128)S(1)}, u32[]{:S(2)}, u32[]{:S(2)}) collective-permute-start(f32[6,8,1024]{2,1,0:T(8,128)S(1)} %get-tuple-element.10), channel_id=1, source_target_pairs={{1,0},{2,1},{3,2},{5,4},{6,5},{7,6},{9,8},{10,9},{11,10},{13,12},{... | collective-permute-start | bytes 589832 | tf_op jit(solution)/shard_map/ppermute | solution.py:223
  17.4 0.7 copy-start.6
  20.6 0.8 copy-start.2
  20.7 0.7 copy-start.3
  21.8 0.7 copy-start
  22.8 40.2 %collective-permute-start = (f32[6,8,1024]{2,1,0:T(8,128)S(1)}, f32[6,8,1024]{2,1,0:T(8,128)S(1)}, u32[]{:S(2)}, u32[]{:S(2)}) collective-permute-start(f32[6,8,1024]{2,1,0:T(8,128)S(1)} %get-tuple-element.11), channel_id=1, source_target_pairs={{0,1},{1,2},{2,3},{4,5},{5,6},{6,7},{8,9},{9,10},{10,11},{12,13},{... | collective-permute-start | bytes 589832 | tf_op jit(solution)/shard_map/ppermute | solution.py:222
  26.8 6.9 %collective-permute-start.6 = (f32[3,8,4,256]{3,2,1,0:T(4,128)S(1)}, f32[3,8,4,256]{3,2,1,0:T(4,128)S(1)}, u32[]{:S(2)}, u32[]{:S(2)}) collective-permute-start(f32[3,8,4,256]{3,2,1,0:T(4,128)S(1)} %get-tuple-element.16), channel_id=1, source_target_pairs={{0,48},{16,0},{32,16},{48,32},{1,49},{17,1},{33,17},{49,33},{2,50}... | collective-permute-start | bytes 294920 | tf_op jit(solution)/shard_map/ppermute | solution.py:206
  29.4 7.4 %collective-permute-start.8 = (f32[3,8,4,256]{3,2,1,0:T(4,128)S(1)}, f32[3,8,4,256]{3,2,1,0:T(4,128)S(1)}, u32[]{:S(2)}, u32[]{:S(2)}) collective-permute-start(f32[3,8,4,256]{3,2,1,0:T(4,128)S(1)} %get-tuple-element.17), channel_id=1, source_target_pairs={{0,16},{16,32},{32,48},{48,0},{1,17},{17,33},{33,49},{49,1},{2,18}... | collective-permute-start | bytes 294920 | tf_op jit(solution)/shard_map/ppermute | solution.py:206
  29.4 7.4 %collective-permute-start.7 = (f32[3,8,4,256]{3,2,1,0:T(4,128)S(1)}, f32[3,8,4,256]{3,2,1,0:T(4,128)S(1)}, u32[]{:S(2)}, u32[]{:S(2)}) collective-permute-start(f32[3,8,4,256]{3,2,1,0:T(4,128)S(1)} %get-tuple-element.18), channel_id=1, source_target_pairs={{0,32},{16,48},{32,0},{48,16},{1,33},{17,49},{33,1},{49,17},{2,34}... | collective-permute-start | bytes 294920 | tf_op jit(solution)/shard_map/ppermute | solution.py:206
  36.8 12.0 %collective-permute-start.11 = (f32[3,8,4,256]{3,2,1,0:T(4,128)S(1)}, f32[3,8,4,256]{3,2,1,0:T(4,128)S(1)}, u32[]{:S(2)}, u32[]{:S(2)}) collective-permute-start(f32[3,8,4,256]{3,2,1,0:T(4,128)S(1)} %pad_maximum_fusion.2), channel_id=1, source_target_pairs={{0,64},{64,128},{128,192},{192,0},{1,65},{65,129},{129,193},{193,1... | collective-permute-start | bytes 294920 | tf_op jit(solution)/shard_map/ppermute | solution.py:177
  39.9 10.7 %collective-permute-start.10 = (f32[3,8,4,256]{3,2,1,0:T(4,128)S(1)}, f32[3,8,4,256]{3,2,1,0:T(4,128)S(1)}, u32[]{:S(2)}, u32[]{:S(2)}) collective-permute-start(f32[3,8,4,256]{3,2,1,0:T(4,128)S(1)} %pad_maximum_fusion.2), channel_id=1, source_target_pairs={{0,128},{64,192},{128,0},{192,64},{1,129},{65,193},{129,1},{193,65... | collective-permute-start | bytes 294920 | tf_op jit(solution)/shard_map/ppermute | solution.py:177
  44.5 7.3 %collective-permute-start.9 = (f32[3,8,4,256]{3,2,1,0:T(4,128)S(1)}, f32[3,8,4,256]{3,2,1,0:T(4,128)S(1)}, u32[]{:S(2)}, u32[]{:S(2)}) collective-permute-start(f32[3,8,4,256]{3,2,1,0:T(4,128)S(1)} %pad_maximum_fusion.2), channel_id=1, source_target_pairs={{0,192},{64,0},{128,64},{192,128},{1,193},{65,1},{129,65},{193,129... | collective-permute-start | bytes 294920 | tf_op jit(solution)/shard_map/ppermute | solution.py:177
  51.9 6.5 %collective-permute-start.14 = (f32[3,8,4,256]{3,2,1,0:T(4,128)S(1)}, f32[3,8,4,256]{3,2,1,0:T(4,128)S(1)}, u32[]{:S(2)}, u32[]{:S(2)}) collective-permute-start(f32[3,8,4,256]{3,2,1,0:T(4,128)S(1)} %pad_maximum_fusion.3), channel_id=1, source_target_pairs={{0,16},{16,32},{32,48},{48,0},{1,17},{17,33},{33,49},{49,1},{2,18}... | collective-permute-start | bytes 294920 | tf_op jit(solution)/shard_map/ppermute | solution.py:177
  52.3 6.1 %collective-permute-start.13 = (f32[3,8,4,256]{3,2,1,0:T(4,128)S(1)}, f32[3,8,4,256]{3,2,1,0:T(4,128)S(1)}, u32[]{:S(2)}, u32[]{:S(2)}) collective-permute-start(f32[3,8,4,256]{3,2,1,0:T(4,128)S(1)} %pad_maximum_fusion.3), channel_id=1, source_target_pairs={{0,32},{16,48},{32,0},{48,16},{1,33},{17,49},{33,1},{49,17},{2,34}... | collective-permute-start | bytes 294920 | tf_op jit(solution)/shard_map/ppermute | solution.py:177
  54.1 4.8 %collective-permute-start.12 = (f32[3,8,4,256]{3,2,1,0:T(4,128)S(1)}, f32[3,8,4,256]{3,2,1,0:T(4,128)S(1)}, u32[]{:S(2)}, u32[]{:S(2)}) collective-permute-start(f32[3,8,4,256]{3,2,1,0:T(4,128)S(1)} %pad_maximum_fusion.3), channel_id=1, source_target_pairs={{0,48},{16,0},{32,16},{48,32},{1,49},{17,1},{33,17},{49,33},{2,50}... | collective-permute-start | bytes 294920 | tf_op jit(solution)/shard_map/ppermute | solution.py:177
  56.1 0.7 copy-start.4
  56.9 0.7 copy-start.5
  59.0 8.4 %collective-permute-start.17 = (f32[3,8,4,1024]{3,2,1,0:T(4,128)S(1)}, f32[3,8,4,1024]{3,2,1,0:T(4,128)S(1)}, u32[]{:S(2)}, u32[]{:S(2)}) collective-permute-start(f32[3,8,4,1024]{3,2,1,0:T(4,128)S(1)} %pad_maximum_fusion.1.r0), channel_id=1, source_target_pairs={{0,12},{4,0},{8,4},{12,8},{1,13},{5,1},{9,5},{13,9},{2,14},{6,2},{... | collective-permute-start | bytes 1179656 | tf_op jit(solution)/shard_map/ppermute | solution.py:177
  60.6 10.0 %collective-permute-start.16 = (f32[3,8,4,1024]{3,2,1,0:T(4,128)S(1)}, f32[3,8,4,1024]{3,2,1,0:T(4,128)S(1)}, u32[]{:S(2)}, u32[]{:S(2)}) collective-permute-start(f32[3,8,4,1024]{3,2,1,0:T(4,128)S(1)} %pad_maximum_fusion.1.r0), channel_id=1, source_target_pairs={{0,8},{4,12},{8,0},{12,4},{1,9},{5,13},{9,1},{13,5},{2,10},{6,14},... | collective-permute-start | bytes 1179656 | tf_op jit(solution)/shard_map/ppermute | solution.py:177
  61.8 19.8 %collective-permute-start.15 = (f32[3,8,4,1024]{3,2,1,0:T(4,128)S(1)}, f32[3,8,4,1024]{3,2,1,0:T(4,128)S(1)}, u32[]{:S(2)}, u32[]{:S(2)}) collective-permute-start(f32[3,8,4,1024]{3,2,1,0:T(4,128)S(1)} %pad_maximum_fusion.1.r0), channel_id=1, source_target_pairs={{0,4},{4,8},{8,12},{12,0},{1,5},{5,9},{9,13},{13,1},{2,6},{6,10},{... | collective-permute-start | bytes 1179656 | tf_op jit(solution)/shard_map/ppermute | solution.py:177

commit v2 on v1

--- a/solution.py
+++ b/solution.py
@@ -38,8 +38,8 @@
     return down, up
 
 
-def kernel(place, own, low, high, r0, r1, r2, r3, wp, wb, wm, wm2, wo, b_in, b_mid, out,
-           st, base, pp, bp, part, gz, bias):
+def kernel(place, own, low, high, r0, r1, r2, r3, wp, wb, wm, wo, b_in, b_mid, out,
+           st, base, pp, bp, part, gz, bias, mid_in, out_in):
     f32, bf16 = jnp.float32, jnp.bfloat16
     lane = lax.broadcasted_iota(jnp.int32, (8, LANES), 1)
     column = lane % NH
@@ -50,7 +50,7 @@
 
     st[0:HALO] = low[...]
     st[HALO : HALO + PLANES] = own[...]
-    st[HALO + PLANES :] = high[...]
+    st[HALO + PLANES : EXT] = high[...]
     bias[0] = jnp.broadcast_to(b_in[...], (UNITS, CHUNK))
     bias[1] = jnp.broadcast_to(b_mid[...], (UNITS, CHUNK))
     pad = jnp.zeros((8, LANES), f32)
@@ -58,6 +58,63 @@
     def inside(e):
         level = slab * PLANES + e - HALO
         return jnp.logical_and(level >= 0, level < slabs * PLANES)
+
+    def patches(e):
+        mid = [st[e, :, k * LANES : (k + 1) * LANES] for k in range(parts)]
+        moved = [shift_y(v, column) for v in mid]
+        rows = []
+        thirds = [[m[0] for m in moved], mid, [m[1] for m in moved]]
+        moved_x = [shift_x(third, lane) for third in thirds]
+        for xed in range(3):
+            for yed in range(3):
+                rows.append(thirds[yed] if xed == 1 else moved_x[yed][xed // 2])
+        for t in range(5):
+            for k in range(parts):
+                second = rows[2 * t + 1][k] if 2 * t + 1 < 9 else pad
+                pair = jnp.concatenate([rows[2 * t][k], second], axis=0)
+                pp[e, 16 * t : 16 * t + 16, k * LANES : (k + 1) * LANES] = pair.astype(bf16)
+        mid = [base[e + SHIFT, :, k * LANES : (k + 1) * LANES] for k in range(parts)]
+        both = []
+        for v in mid:
+            down, up = shift_y(v, column)
+            both.append(jnp.where(upper, down, up))
+        both_down, both_up = shift_x(both, lane)
+        mid_down, mid_up = shift_x(mid, lane)
+        sides = [jnp.where(upper, a, b) for a, b in zip(mid_down, mid_up)]
+        rows = [both_down, both, both_up, sides, mid, [pad] * parts]
+        for t in range(3):
+            for k in range(parts):
+                pair = jnp.concatenate([rows[2 * t][k], rows[2 * t + 1][k]], axis=0)
+                bp[e, 16 * t : 16 * t + 16, k * LANES : (k + 1) * LANES] = pair.astype(bf16)
+
+    def layer_one(e, cells):
+        patch = pp[pl.ds(e - 1, 3), :, cells].reshape(3 * PROWS, CHUNK)
+        base_patch = bp[pl.ds(e - 1, 3), :, cells].reshape(3 * BROWS, CHUNK)
+        first = jnp.tanh(jnp.dot(wb[...], base_patch, preferred_element_type=f32) + bias[0])
+        slope = 1.0 - first * first
+        lin = jnp.dot(wp[...], patch, preferred_element_type=f32)
+        mid_in[0:UNITS, cells] = first.astype(bf16)
+        mid_in[UNITS : 2 * UNITS, cells] = (slope * lin[:UNITS]).astype(bf16)
+        mid_in[2 * UNITS :, cells] = (slope * lin[UNITS:]).astype(bf16)
+
+    def layer_two(cells):
+        lin = jnp.dot(wm[...], mid_in[:, cells], preferred_element_type=f32)
+        second = jnp.tanh(lin[:UNITS] + bias[1])
+        slope = 1.0 - second * second
+        out_in[0:UNITS, cells] = (slope * lin[UNITS : 2 * UNITS]).astype(bf16)
+        out_in[UNITS:, cells] = (slope * lin[2 * UNITS :]).astype(bf16)
+
+    def layer_three(e, cells, keep):
+        stress = jnp.dot(wo[...], out_in[:, cells], preferred_element_type=f32)
+        stress = jnp.where(keep, stress, 0.0)
+        v = st[e, :, cells]
+        u = base[e + SHIFT, :, cells]
+        g = []
+        for j in range(3):
+            u_j = base[e + SHIFT, j : j + 1, cells]
+            v_j = jnp.where(upper_wide, st[e, j : j + 1, cells], st[e, 4 + j : 5 + j, cells])
+            g.append(stress[8 * j : 8 * j + 8] - (u_j * v + v_j * u))
+        return g
 
     for step in range(STEPS):
         lo, hi = 2 * step, EXT - 2 * step
@@ -71,82 +128,59 @@
                 base[start + z, 0:4] = rows
                 base[start + z, 4:8] = rows
 
-        @pl.loop(lo, hi)
-        def _(e):
-            mid = [st[e, :, k * LANES : (k + 1) * LANES] for k in range(parts)]
-            moved = [shift_y(v, column) for v in mid]
-            rows = []
-            thirds = [[m[0] for m in moved], mid, [m[1] for m in moved]]
-            moved_x = [shift_x(third, lane) for third in thirds]
-            for xed in range(3):
-                for yed in range(3):
-                    rows.append(thirds[yed] if xed == 1 else moved_x[yed][xed // 2])
-            for t in range(5):
-                for k in range(parts):
-                    second = rows[2 * t + 1][k] if 2 * t + 1 < 9 else pad
-                    pair = jnp.concatenate([rows[2 * t][k], second], axis=0)
-                    pp[e, 16 * t : 16 * t + 16, k * LANES : (k + 1) * LANES] = pair.astype(bf16)
-            mid = [base[e + SHIFT, :, k * LANES : (k + 1) * LANES] for k in range(parts)]
-            both = []
-            for v in mid:
-                down, up = shift_y(v, column)
-                both.append(jnp.where(upper, down, up))
-            both_down, both_up = shift_x(both, lane)
-            mid_down, mid_up = shift_x(mid, lane)
-            sides = [jnp.where(upper, a, b) for a, b in zip(mid_down, mid_up)]
-            rows = [both_down, both, both_up, sides, mid, [pad] * parts]
-            for t in range(3):
-                for k in range(parts):
-                    pair = jnp.concatenate([rows[2 * t][k], rows[2 * t + 1][k]], axis=0)
-                    bp[e, 16 * t : 16 * t + 16, k * LANES : (k + 1) * LANES] = pair.astype(bf16)
-
-        @pl.loop(lo + 1, hi - 1)
-        def _(e):
-            keep = inside(e)
-            gx, gy = [], []
-            for n in range(PLANE // CHUNK):
-                cells = slice(n * CHUNK, (n + 1) * CHUNK)
-                patch = pp[pl.ds(e - 1, 3), :, cells].reshape(3 * PROWS, CHUNK)
-                base_patch = bp[pl.ds(e - 1, 3), :, cells].reshape(3 * BROWS, CHUNK)
-                first = jnp.tanh(jnp.dot(wb[...], base_patch, preferred_element_type=f32) + bias[0])
-                second = jnp.tanh(
-                    jnp.dot(wm[...], first.astype(bf16), preferred_element_type=f32) + bias[1]
-                )
-                slope_first = 1.0 - first * first
-                slope_second = 1.0 - second * second
-                lin_one = jnp.dot(wp[...], patch, preferred_element_type=f32)
-                lift_one = jnp.concatenate(
-                    [slope_first * lin_one[:UNITS], slope_first * lin_one[UNITS:]], axis=0
-                ).astype(bf16)
-                lin_two = jnp.dot(wm2[...], lift_one, preferred_element_type=f32)
-                lift_two = jnp.concatenate(
-                    [slope_second * lin_two[:UNITS], slope_second * lin_two[UNITS:]], axis=0
-                ).astype(bf16)
-                stress = jnp.dot(wo[...], lift_two, preferred_element_type=f32)
-                stress = jnp.where(keep, stress, 0.0)
-                v = st[e, :, cells]
-                u = base[e + SHIFT, :, cells]
-                g = []
-                for j in range(3):
-                    u_j = base[e + SHIFT, j : j + 1, cells]
-                    v_j = jnp.where(upper_wide, st[e, j : j + 1, cells], st[e, 4 + j : 5 + j, cells])
-                    g.append(stress[8 * j : 8 * j + 8] - (u_j * v + v_j * u))
-                gz[e, :, cells] = g[2]
-                for half in range(CHUNK // LANES):
-                    gx.append(g[0][:, half * LANES : (half + 1) * LANES])
-                    gy.append(g[1][:, half * LANES : (half + 1) * LANES])
+        def divergence(e, gx, gy):
             down_x, up_x = shift_x(gx, lane)
             for k in range(parts):
                 down_y, up_y = shift_y(gy[k], column)
                 part[e, :, k * LANES : (k + 1) * LANES] = (up_x[k] - down_x[k]) + (up_y - down_y)
 
-        @pl.loop(lo + 2, hi - 2)
-        def _(e):
+        def update(e):
             new = st[e] + TIME_STEP * (part[e] + (gz[e + 1] - gz[e - 1]))
             if step == STEPS - 1:
-                out[e - HALO] = new
+                out[jnp.clip(e - HALO, 0, PLANES - 1)] = new
             else:
                 st[e] = jnp.where(inside(e), new, 0.0)
+
+        def body(i, ahead, one, two, three, after):
+            gx, gy = [], []
+            for n in range(PLANE // CHUNK):
+                cells = slice(n * CHUNK, (n + 1) * CHUNK)
+                if three:
+                    g = layer_three(i - 4, cells, inside(i - 4))
+                    gz[i - 4, :, cells] = g[2]
+                    for half in range(CHUNK // LANES):
+                        gx.append(g[0][:, half * LANES : (half + 1) * LANES])
+                        gy.append(g[1][:, half * LANES : (half + 1) * LANES])
+                if two:
+                    layer_two(cells)
+                if one:
+                    layer_one(i - 2, cells)
+            if three:
+                divergence(i - 4, gx, gy)
+            if ahead:
+                patches(i)
+            if after:
+                update(i - 6)
+
+        @pl.loop(lo, lo + 3)
+        def _(i):
+            body(i, True, False, False, False, False)
+
+        body(lo + 3, True, True, False, False, False)
+        body(lo + 4, True, True, True, False, False)
+
+        @pl.loop(lo + 5, lo + 8)
+        def _(i):
+            body(i, True, True, True, True, False)
+
+        @pl.loop(lo + 8, hi)
+        def _(i):
+            body(i, True, True, True, True, True)
+
+        body(hi, False, True, True, True, True)
+        body(hi + 1, False, False, True, True, True)
+        body(hi + 2, False, False, False, True, True)
+        body(hi + 3, False, False, False, False, True)
 
 
 def weights_of(w_in, w_mid, w_out):
@@ -157,12 +191,13 @@
     wp = wp.reshape(2 * UNITS, 3 * PROWS)
     order = (0, 2, 3, 5, 6, 8, 1, 7, 4, 9, 9, 9)
     wb = jnp.concatenate([split[:, :, i : i + 1] for i in order], axis=2).reshape(UNITS, 3 * BROWS)
-    wm2 = (eye[:, None, :, None] * w_mid[None, :, None, :]).reshape(2 * UNITS, 2 * UNITS)
+    wm = jnp.eye(3, dtype=bf16)[:, None, :, None] * w_mid[None, :, None, :]
+    wm = wm.reshape(3 * UNITS, 3 * UNITS)
     out_pad = jnp.pad(w_out, ((0, 1), (0, 0)))
     comps = (0, 3, 4, 6, 3, 1, 5, 6, 4, 5, 2, 6)
     rows = jnp.concatenate([out_pad[i : i + 1] for i in comps], axis=0).reshape(3, 1, 4, 1, UNITS)
     wo = (rows * eye[None, :, None, :, None]).reshape(24, 2 * UNITS)
-    return wp, wb, w_mid, wm2, wo
+    return wp, wb, wm, wo
 
 
 def pick(options, which):
@@ -228,7 +263,7 @@
     new = pl.pallas_call(
         kernel,
         out_shape=jax.ShapeDtypeStruct((PLANES, 8, PLANE), f32),
-        in_specs=[pl.BlockSpec(memory_space=pltpu.SMEM)] + [vmem] * 14,
+        in_specs=[pl.BlockSpec(memory_space=pltpu.SMEM)] + [vmem] * 13,
         out_specs=vmem,
         scratch_shapes=[
             pltpu.VMEM((EXT, 8, PLANE), f32),
@@ -238,6 +273,8 @@
             pltpu.VMEM((EXT, 8, PLANE), f32),
             pltpu.VMEM((EXT, 8, PLANE), f32),
             pltpu.VMEM((2, UNITS, CHUNK), f32),
+            pltpu.VMEM((3 * UNITS, PLANE), bf16),
+            pltpu.VMEM((2 * UNITS, PLANE), bf16),
         ],
         compiler_params=pltpu.CompilerParams(vmem_limit_bytes=40 * 2**20),
     )(place, state, low, high, *come, *weights_of(w_in, w_mid, w_out), b_in[:, None], b_mid[:, None])

time: 202 us -> 118 us (0.58)
  Pallas kernels: 118 us -> 34.7 us
    pallas_call x1, Pallas kernels: 118 us -> 34.7 us  [local(): pl.pallas_call(kernel, out_shape=jax.ShapeDtypeStruct((PLANES, 8, PLANE),...]
  transfers between devices with their start and end apart: 18 -> 18, of which waited for: 8 -> 8; matrix products, arithmetic and copies ran while one was open for 2% -> 3% of each run, Pallas kernels for 0% -> 0%
where the time goes in v2:
time: 118 us; the launch traced here: 117 us
  starting transfers between devices  41.3 us (35%)
  Pallas kernels  34.7 us (29%)
  waiting for transfers between devices  25.6 us (22%)
  local copies, waits for them, and re-layouts  8.37 us (7%)
  between operations  6.29 us (5%)
  other arithmetic  1.19 us (1%)
    pallas_call x1, Pallas kernels, local(): pl.pallas_call(kernel, out_shape=jax.ShapeDtypeStruct((PLANES, 8, PLANE),...  34.7 us
    ppermute x9, waiting for transfers between devices, around(): lax.ppermute(piece, axis, [(i, (i + k) % 4) for i in range(4)])  22.5 us
    ppermute x9, starting transfers between devices, around(): lax.ppermute(piece, axis, [(i, (i + k) % 4) for i in range(4)])  17.6 us
    ppermute x4, starting transfers between devices, spread_base(): come.append(lax.ppermute(send, ('y', 'gz'), pairs))  13.8 us
    unnamed x25, local copies, waits for them, and re-layouts  4.57 us
    ppermute x3, starting transfers between devices, spread_base(): come.append(lax.ppermute(cells_of((x + k) % 4), 'x', pairs))  4.29 us
    ppermute x1, starting transfers between devices, local(): low = lax.ppermute(state[PLANES - HALO:], 'gz', up)  3.64 us
    ppermute x3, waiting for transfers between devices, spread_base(): come.append(lax.ppermute(cells_of((x + k) % 4), 'x', pairs))  3.03 us
  transfers between devices with their start and end apart: 18, of which 8 were waited for; matrix products, arithmetic and copies ran while one was open for 3% of the time, Pallas kernels for 0%

profile of v2, /device:TPU:1, one launch (start us, length us, event | category | flops | bytes accessed | tf_op | source)
XLA Modules:
  0.0 117.4 jit_solution(9424062949714555482)
XLA Ops:
  0.0 1.1 copy.15
  1.3 5.1 %collective-permute-start.5 = (f32[8,4,1024]{2,1,0:T(4,128)S(1)}, f32[8,4,1024]{2,1,0:T(4,128)S(1)}, u32[]{:S(2)}, u32[]{:S(2)}) collective-permute-start(f32[8,4,1024]{2,1,0:T(4,128)S(1)} %get-tuple-element.21), channel_id=1, source_target_pairs={{0,1},{1,2},{2,3},{4,4},{5,5},{6,6},{7,7},{8,8},{9,9},{10,10},{11,... | collective-permute-start | bytes 393224 | tf_op jit(solution)/shard_map/ppermute | solution.py:231
  6.3 1.9 %collective-permute-start.4 = (f32[8,4,1024]{2,1,0:T(4,128)S(1)}, f32[8,4,1024]{2,1,0:T(4,128)S(1)}, u32[]{:S(2)}, u32[]{:S(2)}) collective-permute-start(f32[8,4,1024]{2,1,0:T(4,128)S(1)} %get-tuple-element.22), channel_id=1, source_target_pairs={{12,1},{13,2},{14,3},{0,4},{1,5},{2,6},{3,7},{4,8},{5,9},{6,10},{7... | collective-permute-start | bytes 393224 | tf_op jit(solution)/shard_map/ppermute | solution.py:231
  8.3 4.9 %collective-permute-start.2 = (f32[8,4,1024]{2,1,0:T(4,128)S(1)}, f32[8,4,1024]{2,1,0:T(4,128)S(1)}, u32[]{:S(2)}, u32[]{:S(2)}) collective-permute-start(f32[8,4,1024]{2,1,0:T(4,128)S(1)} %get-tuple-element.23), channel_id=1, source_target_pairs={{4,1},{5,2},{6,3},{8,4},{9,5},{10,6},{11,7},{12,8},{13,9},{14,10},... | collective-permute-start | bytes 393224 | tf_op jit(solution)/shard_map/ppermute | solution.py:231
  13.1 1.9 %collective-permute-start.3 = (f32[8,4,1024]{2,1,0:T(4,128)S(1)}, f32[8,4,1024]{2,1,0:T(4,128)S(1)}, u32[]{:S(2)}, u32[]{:S(2)}) collective-permute-start(f32[8,4,1024]{2,1,0:T(4,128)S(1)} %get-tuple-element.24), channel_id=1, source_target_pairs={{8,1},{9,2},{10,3},{12,4},{13,5},{14,6},{15,7},{0,8},{1,9},{2,10},... | collective-permute-start | bytes 393224 | tf_op jit(solution)/shard_map/ppermute | solution.py:231
  15.4 1.9 %collective-permute-start.1 = (f32[6,8,1024]{2,1,0:T(8,128)S(1)}, f32[6,8,1024]{2,1,0:T(8,128)S(1)}, u32[]{:S(2)}, u32[]{:S(2)}) collective-permute-start(f32[6,8,1024]{2,1,0:T(8,128)S(1)} %get-tuple-element.10), channel_id=1, source_target_pairs={{1,0},{2,1},{3,2},{5,4},{6,5},{7,6},{9,8},{10,9},{11,10},{13,12},{... | collective-permute-start | bytes 589832 | tf_op jit(solution)/shard_map/ppermute | solution.py:258
  17.4 0.6 copy-done.6
  18.1 0.6 fusion.19
  20.7 0.7 copy-done.3
  22.9 3.6 %collective-permute-start = (f32[6,8,1024]{2,1,0:T(8,128)S(1)}, f32[6,8,1024]{2,1,0:T(8,128)S(1)}, u32[]{:S(2)}, u32[]{:S(2)}) collective-permute-start(f32[6,8,1024]{2,1,0:T(8,128)S(1)} %get-tuple-element.11), channel_id=1, source_target_pairs={{0,1},{1,2},{2,3},{4,5},{5,6},{6,7},{8,9},{9,10},{10,11},{12,13},{... | collective-permute-start | bytes 589832 | tf_op jit(solution)/shard_map/ppermute | solution.py:257
  26.9 2.6 %collective-permute-start.6 = (f32[3,8,4,256]{3,2,1,0:T(4,128)S(1)}, f32[3,8,4,256]{3,2,1,0:T(4,128)S(1)}, u32[]{:S(2)}, u32[]{:S(2)}) collective-permute-start(f32[3,8,4,256]{3,2,1,0:T(4,128)S(1)} %get-tuple-element.16), channel_id=1, source_target_pairs={{0,48},{16,0},{32,16},{48,32},{1,49},{17,1},{33,17},{49,33},{2,50}... | collective-permute-start | bytes 294920 | tf_op jit(solution)/shard_map/ppermute | solution.py:241
  29.4 1.7 %collective-permute-start.7 = (f32[3,8,4,256]{3,2,1,0:T(4,128)S(1)}, f32[3,8,4,256]{3,2,1,0:T(4,128)S(1)}, u32[]{:S(2)}, u32[]{:S(2)}) collective-permute-start(f32[3,8,4,256]{3,2,1,0:T(4,128)S(1)} %get-tuple-element.18), channel_id=1, source_target_pairs={{0,32},{16,48},{32,0},{48,16},{1,33},{17,49},{33,1},{49,17},{2,34}... | collective-permute-start | bytes 294920 | tf_op jit(solution)/shard_map/ppermute | solution.py:241
  31.1 0.7 fusion.17
  33.8 3.0 %collective-permute-done.8 = f32[3,8,4,256]{3,2,1,0:T(4,128)S(1)} collective-permute-done((f32[3,8,4,256]{3,2,1,0:T(4,128)S(1)}, f32[3,8,4,256]{3,2,1,0:T(4,128)S(1)}, u32[]{:S(2)}, u32[]{:S(2)}) %collective-permute-start.8) | collective-permute-done | bytes 98336 | tf_op jit(solution)/shard_map/ppermute | solution.py:241
  36.9 3.1 %collective-permute-start.11 = (f32[3,8,4,256]{3,2,1,0:T(4,128)S(1)}, f32[3,8,4,256]{3,2,1,0:T(4,128)S(1)}, u32[]{:S(2)}, u32[]{:S(2)}) collective-permute-start(f32[3,8,4,256]{3,2,1,0:T(4,128)S(1)} %pad_maximum_fusion.2), channel_id=1, source_target_pairs={{0,64},{64,128},{128,192},{192,0},{1,65},{65,129},{129,193},{193,1... | collective-permute-start | bytes 294920 | tf_op jit(solution)/shard_map/ppermute | solution.py:212
  40.0 4.6 %collective-permute-start.10 = (f32[3,8,4,256]{3,2,1,0:T(4,128)S(1)}, f32[3,8,4,256]{3,2,1,0:T(4,128)S(1)}, u32[]{:S(2)}, u32[]{:S(2)}) collective-permute-start(f32[3,8,4,256]{3,2,1,0:T(4,128)S(1)} %pad_maximum_fusion.2), channel_id=1, source_target_pairs={{0,128},{64,192},{128,0},{192,64},{1,129},{65,193},{129,1},{193,65... | collective-permute-start | bytes 294920 | tf_op jit(solution)/shard_map/ppermute | solution.py:212
  44.5 2.4 %collective-permute-start.9 = (f32[3,8,4,256]{3,2,1,0:T(4,128)S(1)}, f32[3,8,4,256]{3,2,1,0:T(4,128)S(1)}, u32[]{:S(2)}, u32[]{:S(2)}) collective-permute-start(f32[3,8,4,256]{3,2,1,0:T(4,128)S(1)} %pad_maximum_fusion.2), channel_id=1, source_target_pairs={{0,192},{64,0},{128,64},{192,128},{1,193},{65,1},{129,65},{193,129... | collective-permute-start | bytes 294920 | tf_op jit(solution)/shard_map/ppermute | solution.py:212
  48.9 1.8 %collective-permute-done.10 = f32[3,8,4,256]{3,2,1,0:T(4,128)S(1)} collective-permute-done((f32[3,8,4,256]{3,2,1,0:T(4,128)S(1)}, f32[3,8,4,256]{3,2,1,0:T(4,128)S(1)}, u32[]{:S(2)}, u32[]{:S(2)}) %collective-permute-start.10) | collective-permute-done | bytes 98336 | tf_op jit(solution)/shard_map/ppermute | solution.py:212
  50.7 1.2 %collective-permute-done.9 = f32[3,8,4,256]{3,2,1,0:T(4,128)S(1)} collective-permute-done((f32[3,8,4,256]{3,2,1,0:T(4,128)S(1)}, f32[3,8,4,256]{3,2,1,0:T(4,128)S(1)}, u32[]{:S(2)}, u32[]{:S(2)}) %collective-permute-start.9) | collective-permute-done | bytes 98336 | tf_op jit(solution)/shard_map/ppermute | solution.py:212
  52.3 1.8 %collective-permute-start.13 = (f32[3,8,4,256]{3,2,1,0:T(4,128)S(1)}, f32[3,8,4,256]{3,2,1,0:T(4,128)S(1)}, u32[]{:S(2)}, u32[]{:S(2)}) collective-permute-start(f32[3,8,4,256]{3,2,1,0:T(4,128)S(1)} %pad_maximum_fusion.3), channel_id=1, source_target_pairs={{0,32},{16,48},{32,0},{48,16},{1,33},{17,49},{33,1},{49,17},{2,34}... | collective-permute-start | bytes 294920 | tf_op jit(solution)/shard_map/ppermute | solution.py:212
  54.1 2.0 %collective-permute-start.12 = (f32[3,8,4,256]{3,2,1,0:T(4,128)S(1)}, f32[3,8,4,256]{3,2,1,0:T(4,128)S(1)}, u32[]{:S(2)}, u32[]{:S(2)}) collective-permute-start(f32[3,8,4,256]{3,2,1,0:T(4,128)S(1)} %pad_maximum_fusion.3), channel_id=1, source_target_pairs={{0,48},{16,0},{32,16},{48,32},{1,49},{17,1},{33,17},{49,33},{2,50}... | collective-permute-start | bytes 294920 | tf_op jit(solution)/shard_map/ppermute | solution.py:212
  56.2 0.7 copy-done.4
  56.9 0.7 copy-done.5
  57.7 0.7 collective-permute-done.14
  59.1 1.5 %collective-permute-start.17 = (f32[3,8,4,1024]{3,2,1,0:T(4,128)S(1)}, f32[3,8,4,1024]{3,2,1,0:T(4,128)S(1)}, u32[]{:S(2)}, u32[]{:S(2)}) collective-permute-start(f32[3,8,4,1024]{3,2,1,0:T(4,128)S(1)} %pad_maximum_fusion.1.r0), channel_id=1, source_target_pairs={{0,12},{4,0},{8,4},{12,8},{1,13},{5,1},{9,5},{13,9},{2,14},{6,2},{... | collective-permute-start | bytes 1179656 | tf_op jit(solution)/shard_map/ppermute | solution.py:212
  60.6 1.2 %collective-permute-start.16 = (f32[3,8,4,1024]{3,2,1,0:T(4,128)S(1)}, f32[3,8,4,1024]{3,2,1,0:T(4,128)S(1)}, u32[]{:S(2)}, u32[]{:S(2)}) collective-permute-start(f32[3,8,4,1024]{3,2,1,0:T(4,128)S(1)} %pad_maximum_fusion.1.r0), channel_id=1, source_target_pairs={{0,8},{4,12},{8,0},{12,4},{1,9},{5,13},{9,1},{13,5},{2,10},{6,14},... | collective-permute-start | bytes 1179656 | tf_op jit(solution)/shard_map/ppermute | solution.py:212
  61.8 0.8 collective-permute-start.15
  63.2 4.3 %collective-permute-done.17.r3 = f32[3,8,4,1024]{3,2,1,0:T(4,128)S(1)} collective-permute-done((f32[3,8,4,1024]{3,2,1,0:T(4,128)S(1)}, f32[3,8,4,1024]{3,2,1,0:T(4,128)S(1)}, u32[]{:S(2)}, u32[]{:S(2)}) %collective-permute-start.17) | collective-permute-done | bytes 393248 | tf_op jit(solution)/shard_map/ppermute | solution.py:212
  67.5 3.1 %collective-permute-done.16.r2 = f32[3,8,4,1024]{3,2,1,0:T(4,128)S(1)} collective-permute-done((f32[3,8,4,1024]{3,2,1,0:T(4,128)S(1)}, f32[3,8,4,1024]{3,2,1,0:T(4,128)S(1)}, u32[]{:S(2)}, u32[]{:S(2)}) %collective-permute-start.16) | collective-permute-done | bytes 393248 | tf_op jit(solution)/shard_map/ppermute | solution.py:212
  70.6 11.0 %collective-permute-done.15.r1 = f32[3,8,4,1024]{3,2,1,0:T(4,128)S(1)} collective-permute-done((f32[3,8,4,1024]{3,2,1,0:T(4,128)S(1)}, f32[3,8,4,1024]{3,2,1,0:T(4,128)S(1)}, u32[]{:S(2)}, u32[]{:S(2)}) %collective-permute-start.15) | collective-permute-done | bytes 393248 | tf_op jit(solution)/shard_map/ppermute | solution.py:212
  81.6 34.7 %shard_map.82 = f32[16,8,1024]{2,1,0:T(8,128)S(1)} custom-call(s32[3]{0:T(128)S(1)} %pad_add_fusion.place, f32[16,8,1024]{2,1,0:T(8,128)S(1)} %bitcast.42, f32[6,8,1024]{2,1,0:T(8,128)S(1)} %collective-permute-done.low, f32[6,8,1024]{2,1,0:T(8,128)S(1)} %collective-permute-done.1.high, f32[3,8,4,1024]{3,2,1,0:T(4,128)S(1)} %pad_maximum_fusion.1.r0, ...), custom_call_target="tpu_custom_call" | custom-call | tf_op jit(solution)/shard_map/pallas_call | solution.py:263
  116.3 1.1 copy.24
  (70 shorter events, 4.2 us)
Async XLA Ops:
  1.1 13.9 %copy-start = (f32[2,4,16,1024]{3,2,1,0:T(8,128)S(1)}, f32[2,4,16,1024]{3,2,1,0:T(8,128)}, u32[]{:S(2)}) copy-start(f32[2,4,16,1024]{3,2,1,0:T(8,128)} %param.9) | copy-start | bytes 1572868
  1.3 21.6 %collective-permute-start.5 = (f32[8,4,1024]{2,1,0:T(4,128)S(1)}, f32[8,4,1024]{2,1,0:T(4,128)S(1)}, u32[]{:S(2)}, u32[]{:S(2)}) collective-permute-start(f32[8,4,1024]{2,1,0:T(4,128)S(1)} %get-tuple-element.21), channel_id=1, source_target_pairs={{0,1},{1,2},{2,3},{4,4},{5,5},{6,6},{7,7},{8,8},{9,9},{10,10},{11,... | collective-permute-start | bytes 393224 | tf_op jit(solution)/shard_map/ppermute | solution.py:231
  6.3 20.2 %collective-permute-start.4 = (f32[8,4,1024]{2,1,0:T(4,128)S(1)}, f32[8,4,1024]{2,1,0:T(4,128)S(1)}, u32[]{:S(2)}, u32[]{:S(2)}) collective-permute-start(f32[8,4,1024]{2,1,0:T(4,128)S(1)} %get-tuple-element.22), channel_id=1, source_target_pairs={{12,1},{13,2},{14,3},{0,4},{1,5},{2,6},{3,7},{4,8},{5,9},{6,10},{7... | collective-permute-start | bytes 393224 | tf_op jit(solution)/shard_map/ppermute | solution.py:231
  8.3 18.3 %collective-permute-start.2 = (f32[8,4,1024]{2,1,0:T(4,128)S(1)}, f32[8,4,1024]{2,1,0:T(4,128)S(1)}, u32[]{:S(2)}, u32[]{:S(2)}) collective-permute-start(f32[8,4,1024]{2,1,0:T(4,128)S(1)} %get-tuple-element.23), channel_id=1, source_target_pairs={{4,1},{5,2},{6,3},{8,4},{9,5},{10,6},{11,7},{12,8},{13,9},{14,10},... | collective-permute-start | bytes 393224 | tf_op jit(solution)/shard_map/ppermute | solution.py:231
  13.1 13.4 %collective-permute-start.3 = (f32[8,4,1024]{2,1,0:T(4,128)S(1)}, f32[8,4,1024]{2,1,0:T(4,128)S(1)}, u32[]{:S(2)}, u32[]{:S(2)}) collective-permute-start(f32[8,4,1024]{2,1,0:T(4,128)S(1)} %get-tuple-element.24), channel_id=1, source_target_pairs={{8,1},{9,2},{10,3},{12,4},{13,5},{14,6},{15,7},{0,8},{1,9},{2,10},... | collective-permute-start | bytes 393224 | tf_op jit(solution)/shard_map/ppermute | solution.py:231
  15.4 47.8 %collective-permute-start.1 = (f32[6,8,1024]{2,1,0:T(8,128)S(1)}, f32[6,8,1024]{2,1,0:T(8,128)S(1)}, u32[]{:S(2)}, u32[]{:S(2)}) collective-permute-start(f32[6,8,1024]{2,1,0:T(8,128)S(1)} %get-tuple-element.10), channel_id=1, source_target_pairs={{1,0},{2,1},{3,2},{5,4},{6,5},{7,6},{9,8},{10,9},{11,10},{13,12},{... | collective-permute-start | bytes 589832 | tf_op jit(solution)/shard_map/ppermute | solution.py:258
  17.4 0.7 copy-start.6
  20.7 0.8 copy-start.1
  20.7 0.7 copy-start.3
  22.0 0.7 copy-start.2
  22.9 40.3 %collective-permute-start = (f32[6,8,1024]{2,1,0:T(8,128)S(1)}, f32[6,8,1024]{2,1,0:T(8,128)S(1)}, u32[]{:S(2)}, u32[]{:S(2)}) collective-permute-start(f32[6,8,1024]{2,1,0:T(8,128)S(1)} %get-tuple-element.11), channel_id=1, source_target_pairs={{0,1},{1,2},{2,3},{4,5},{5,6},{6,7},{8,9},{9,10},{10,11},{12,13},{... | collective-permute-start | bytes 589832 | tf_op jit(solution)/shard_map/ppermute | solution.py:257
  26.9 6.9 %collective-permute-start.6 = (f32[3,8,4,256]{3,2,1,0:T(4,128)S(1)}, f32[3,8,4,256]{3,2,1,0:T(4,128)S(1)}, u32[]{:S(2)}, u32[]{:S(2)}) collective-permute-start(f32[3,8,4,256]{3,2,1,0:T(4,128)S(1)} %get-tuple-element.16), channel_id=1, source_target_pairs={{0,48},{16,0},{32,16},{48,32},{1,49},{17,1},{33,17},{49,33},{2,50}... | collective-permute-start | bytes 294920 | tf_op jit(solution)/shard_map/ppermute | solution.py:241
  29.4 7.4 %collective-permute-start.8 = (f32[3,8,4,256]{3,2,1,0:T(4,128)S(1)}, f32[3,8,4,256]{3,2,1,0:T(4,128)S(1)}, u32[]{:S(2)}, u32[]{:S(2)}) collective-permute-start(f32[3,8,4,256]{3,2,1,0:T(4,128)S(1)} %get-tuple-element.17), channel_id=1, source_target_pairs={{0,16},{16,32},{32,48},{48,0},{1,17},{17,33},{33,49},{49,1},{2,18}... | collective-permute-start | bytes 294920 | tf_op jit(solution)/shard_map/ppermute | solution.py:241
  29.4 7.4 %collective-permute-start.7 = (f32[3,8,4,256]{3,2,1,0:T(4,128)S(1)}, f32[3,8,4,256]{3,2,1,0:T(4,128)S(1)}, u32[]{:S(2)}, u32[]{:S(2)}) collective-permute-start(f32[3,8,4,256]{3,2,1,0:T(4,128)S(1)} %get-tuple-element.18), channel_id=1, source_target_pairs={{0,32},{16,48},{32,0},{48,16},{1,33},{17,49},{33,1},{49,17},{2,34}... | collective-permute-start | bytes 294920 | tf_op jit(solution)/shard_map/ppermute | solution.py:241
  36.9 12.0 %collective-permute-start.11 = (f32[3,8,4,256]{3,2,1,0:T(4,128)S(1)}, f32[3,8,4,256]{3,2,1,0:T(4,128)S(1)}, u32[]{:S(2)}, u32[]{:S(2)}) collective-permute-start(f32[3,8,4,256]{3,2,1,0:T(4,128)S(1)} %pad_maximum_fusion.2), channel_id=1, source_target_pairs={{0,64},{64,128},{128,192},{192,0},{1,65},{65,129},{129,193},{193,1... | collective-permute-start | bytes 294920 | tf_op jit(solution)/shard_map/ppermute | solution.py:212
  40.0 10.7 %collective-permute-start.10 = (f32[3,8,4,256]{3,2,1,0:T(4,128)S(1)}, f32[3,8,4,256]{3,2,1,0:T(4,128)S(1)}, u32[]{:S(2)}, u32[]{:S(2)}) collective-permute-start(f32[3,8,4,256]{3,2,1,0:T(4,128)S(1)} %pad_maximum_fusion.2), channel_id=1, source_target_pairs={{0,128},{64,192},{128,0},{192,64},{1,129},{65,193},{129,1},{193,65... | collective-permute-start | bytes 294920 | tf_op jit(solution)/shard_map/ppermute | solution.py:212
  44.5 7.3 %collective-permute-start.9 = (f32[3,8,4,256]{3,2,1,0:T(4,128)S(1)}, f32[3,8,4,256]{3,2,1,0:T(4,128)S(1)}, u32[]{:S(2)}, u32[]{:S(2)}) collective-permute-start(f32[3,8,4,256]{3,2,1,0:T(4,128)S(1)} %pad_maximum_fusion.2), channel_id=1, source_target_pairs={{0,192},{64,0},{128,64},{192,128},{1,193},{65,1},{129,65},{193,129... | collective-permute-start | bytes 294920 | tf_op jit(solution)/shard_map/ppermute | solution.py:212
  52.0 6.5 %collective-permute-start.14 = (f32[3,8,4,256]{3,2,1,0:T(4,128)S(1)}, f32[3,8,4,256]{3,2,1,0:T(4,128)S(1)}, u32[]{:S(2)}, u32[]{:S(2)}) collective-permute-start(f32[3,8,4,256]{3,2,1,0:T(4,128)S(1)} %pad_maximum_fusion.3), channel_id=1, source_target_pairs={{0,16},{16,32},{32,48},{48,0},{1,17},{17,33},{33,49},{49,1},{2,18}... | collective-permute-start | bytes 294920 | tf_op jit(solution)/shard_map/ppermute | solution.py:212
  52.3 6.1 %collective-permute-start.13 = (f32[3,8,4,256]{3,2,1,0:T(4,128)S(1)}, f32[3,8,4,256]{3,2,1,0:T(4,128)S(1)}, u32[]{:S(2)}, u32[]{:S(2)}) collective-permute-start(f32[3,8,4,256]{3,2,1,0:T(4,128)S(1)} %pad_maximum_fusion.3), channel_id=1, source_target_pairs={{0,32},{16,48},{32,0},{48,16},{1,33},{17,49},{33,1},{49,17},{2,34}... | collective-permute-start | bytes 294920 | tf_op jit(solution)/shard_map/ppermute | solution.py:212
  54.1 4.8 %collective-permute-start.12 = (f32[3,8,4,256]{3,2,1,0:T(4,128)S(1)}, f32[3,8,4,256]{3,2,1,0:T(4,128)S(1)}, u32[]{:S(2)}, u32[]{:S(2)}) collective-permute-start(f32[3,8,4,256]{3,2,1,0:T(4,128)S(1)} %pad_maximum_fusion.3), channel_id=1, source_target_pairs={{0,48},{16,0},{32,16},{48,32},{1,49},{17,1},{33,17},{49,33},{2,50}... | collective-permute-start | bytes 294920 | tf_op jit(solution)/shard_map/ppermute | solution.py:212
  56.2 0.7 copy-start.4
  56.9 0.7 copy-start.5
  59.1 8.4 %collective-permute-start.17 = (f32[3,8,4,1024]{3,2,1,0:T(4,128)S(1)}, f32[3,8,4,1024]{3,2,1,0:T(4,128)S(1)}, u32[]{:S(2)}, u32[]{:S(2)}) collective-permute-start(f32[3,8,4,1024]{3,2,1,0:T(4,128)S(1)} %pad_maximum_fusion.1.r0), channel_id=1, source_target_pairs={{0,12},{4,0},{8,4},{12,8},{1,13},{5,1},{9,5},{13,9},{2,14},{6,2},{... | collective-permute-start | bytes 1179656 | tf_op jit(solution)/shard_map/ppermute | solution.py:212
  60.6 10.0 %collective-permute-start.16 = (f32[3,8,4,1024]{3,2,1,0:T(4,128)S(1)}, f32[3,8,4,1024]{3,2,1,0:T(4,128)S(1)}, u32[]{:S(2)}, u32[]{:S(2)}) collective-permute-start(f32[3,8,4,1024]{3,2,1,0:T(4,128)S(1)} %pad_maximum_fusion.1.r0), channel_id=1, source_target_pairs={{0,8},{4,12},{8,0},{12,4},{1,9},{5,13},{9,1},{13,5},{2,10},{6,14},... | collective-permute-start | bytes 1179656 | tf_op jit(solution)/shard_map/ppermute | solution.py:212
  61.8 19.7 %collective-permute-start.15 = (f32[3,8,4,1024]{3,2,1,0:T(4,128)S(1)}, f32[3,8,4,1024]{3,2,1,0:T(4,128)S(1)}, u32[]{:S(2)}, u32[]{:S(2)}) collective-permute-start(f32[3,8,4,1024]{3,2,1,0:T(4,128)S(1)} %pad_maximum_fusion.1.r0), channel_id=1, source_target_pairs={{0,4},{4,8},{8,12},{12,0},{1,5},{5,9},{9,13},{13,1},{2,6},{6,10},{... | collective-permute-start | bytes 1179656 | tf_op jit(solution)/shard_map/ppermute | solution.py:212

commit v3 on v2

--- a/solution.py
+++ b/solution.py
@@ -1,5 +1,3 @@
-import functools
-
 import jax
 import jax.numpy as jnp
 from jax import lax
@@ -13,8 +11,6 @@
 PLANES = 16
 HALO = 6
 EXT = PLANES + 2 * HALO
-BLOCK = 8
-SHIFT = BLOCK - HALO
 PLANE = 1024
 UNITS = 64
 LANES = 128
@@ -38,7 +34,7 @@
     return down, up
 
 
-def kernel(place, own, low, high, r0, r1, r2, r3, wp, wb, wm, wo, b_in, b_mid, out,
+def kernel(place, own, low, high, base_low, base_own, base_high, wp, wb, wm, wo, b_in, b_mid, out,
            st, base, pp, bp, part, gz, bias, mid_in, out_in):
     f32, bf16 = jnp.float32, jnp.bfloat16
     lane = lax.broadcasted_iota(jnp.int32, (8, LANES), 1)
@@ -46,7 +42,7 @@
     upper = lax.broadcasted_iota(jnp.int32, (8, LANES), 0) < 4
     upper_wide = lax.broadcasted_iota(jnp.int32, (8, CHUNK), 0) < 4
     parts = PLANE // LANES
-    y_now, slab, slabs = place[0], place[1], place[2]
+    slab, slabs = place[0], place[1]
 
     st[0:HALO] = low[...]
     st[HALO : HALO + PLANES] = own[...]
@@ -73,7 +69,7 @@
                 second = rows[2 * t + 1][k] if 2 * t + 1 < 9 else pad
                 pair = jnp.concatenate([rows[2 * t][k], second], axis=0)
                 pp[e, 16 * t : 16 * t + 16, k * LANES : (k + 1) * LANES] = pair.astype(bf16)
-        mid = [base[e + SHIFT, :, k * LANES : (k + 1) * LANES] for k in range(parts)]
+        mid = [base[e, :, k * LANES : (k + 1) * LANES] for k in range(parts)]
         both = []
         for v in mid:
             down, up = shift_y(v, column)
@@ -108,10 +104,10 @@
         stress = jnp.dot(wo[...], out_in[:, cells], preferred_element_type=f32)
         stress = jnp.where(keep, stress, 0.0)
         v = st[e, :, cells]
-        u = base[e + SHIFT, :, cells]
+        u = base[e, :, cells]
         g = []
         for j in range(3):
-            u_j = base[e + SHIFT, j : j + 1, cells]
+            u_j = base[e, j : j + 1, cells]
             v_j = jnp.where(upper_wide, st[e, j : j + 1, cells], st[e, 4 + j : 5 + j, cells])
             g.append(stress[8 * j : 8 * j + 8] - (u_j * v + v_j * u))
         return g
@@ -119,14 +115,18 @@
     for step in range(STEPS):
         lo, hi = 2 * step, EXT - 2 * step
 
-        for k, ref in enumerate((r0, r1, r2, r3)):
-            start = lax.rem(y_now + 4 - k, 4) * BLOCK
-
-            @pl.loop(0, BLOCK)
+        for start, planes, ref in (
+            (0, HALO, base_low),
+            (HALO, PLANES, base_own),
+            (HALO + PLANES, HALO, base_high),
+        ):
+
+            @pl.loop(0, planes)
             def _(z):
-                rows = ref[step, z]
-                base[start + z, 0:4] = rows
-                base[start + z, 4:8] = rows
+                for k in range(parts):
+                    rows = ref[z, step, k]
+                    base[start + z, 0:4, k * LANES : (k + 1) * LANES] = rows
+                    base[start + z, 4:8, k * LANES : (k + 1) * LANES] = rows
 
         def divergence(e, gx, gy):
             down_x, up_x = shift_x(gx, lane)
@@ -200,52 +200,52 @@
     return wp, wb, wm, wo
 
 
-def pick(options, which):
-    chosen = options[0]
-    for k in range(1, len(options)):
-        chosen = jnp.where(which == k, options[k], chosen)
-    return chosen
-
-
-def around(piece, axis):
-    return [piece] + [
-        lax.ppermute(piece, axis, [(i, (i + k) % 4) for i in range(4)]) for k in (1, 2, 3)
+def take_plane(owner, come, mine):
+    for s in range(STEPS):
+        mine[s] = come[owner[s] & 15]
+
+
+def take_copies(owner, place, c0, c1, c2, c3, send):
+    for s in range(STEPS):
+        turn = (place[2] - (owner[s] >> 4)) & 3
+        chosen = jnp.where(turn == 1, c1[s], c0[s])
+        chosen = jnp.where(turn == 2, c2[s], chosen)
+        chosen = jnp.where(turn == 3, c3[s], chosen)
+        for i in range(PLANES):
+            send[i, s] = chosen
+
+
+def spread_base(base_store, owner_steps, place, slabs):
+    f32 = jnp.float32
+    smem, vmem = (pl.BlockSpec(memory_space=m) for m in (pltpu.SMEM, pltpu.VMEM))
+    tiles = jnp.transpose(base_store[0], (1, 0, 2)).reshape(PLANES, 4, 8, LANES)
+    tiles = jnp.transpose(tiles, (0, 2, 1, 3))
+    tiles = tiles.reshape(PLANES, 4, 8, LANES)
+    come = lax.all_to_all(tiles, ("x", "y"), 0, 0, tiled=True)
+    mine = pl.pallas_call(
+        take_plane,
+        out_shape=jax.ShapeDtypeStruct((STEPS, 4, 8, LANES), f32),
+        in_specs=[smem, vmem],
+        out_specs=vmem,
+        compiler_params=pltpu.CompilerParams(vmem_limit_bytes=4 * 2**20),
+    )(owner_steps, come)
+    come = [mine] + [
+        lax.ppermute(mine, "h", [(i, (i + k) % 4) for i in range(4)]) for k in (1, 2, 3)
     ]
-
-
-def spread_base(base_store, owner_steps, slabs):
-    x, y, h = (lax.axis_index(a) for a in ("x", "y", "h"))
-    owner_h, owner_x, owner_y = (owner_steps // 16, (owner_steps // 4) % 4, owner_steps % 4)
-    blocks = jnp.transpose(base_store[0].reshape(4, 2, BLOCK, PLANE), (1, 2, 0, 3))
-    come = []
-    for k in range(4):
-        pairs = []
-        for target in range(4):
-            source = (target - k) % 4
-            for slab in range(slabs):
-                other = slab + (-1, 0, 0, 1)[target]
-                if 0 <= other < slabs:
-                    pairs.append((source * slabs + other, target * slabs + slab))
-        target = (y + k) % 4
-        send = jnp.where(target % 2 == 0, blocks[1], blocks[0])
-        come.append(lax.ppermute(send, ("y", "gz"), pairs))
-    mine = jnp.stack([pick(come, (y - owner_y[s]) % 4) for s in range(STEPS)])
-    width = PLANE // 4
-
-    def cells_of(which):
-        return lax.dynamic_slice_in_dim(mine, which * width, width, axis=3)
-
-    come = [cells_of(x)]
-    for k in (1, 2, 3):
-        pairs = [(i, (i + k) % 4) for i in range(4)]
-        come.append(lax.ppermute(cells_of((x + k) % 4), "x", pairs))
-    mine = jnp.stack([pick([c[s] for c in come], (x - owner_x[s]) % 4) for s in range(STEPS)])
-    come = around(mine, "h")
-    mine = jnp.stack([pick([c[s] for c in come], (h - owner_h[s]) % 4) for s in range(STEPS)])
-    come = around(mine, "x")
-    ring = [come[0], come[3], come[2], come[1]]
-    whole = jnp.concatenate([pick([ring[(j - i) % 4] for i in range(4)], x) for j in range(4)], axis=3)
-    return around(whole, "y")
+    send = pl.pallas_call(
+        take_copies,
+        out_shape=jax.ShapeDtypeStruct((PLANES, STEPS, 4, 8, LANES), f32),
+        in_specs=[smem, smem] + [vmem] * 4,
+        out_specs=vmem,
+        compiler_params=pltpu.CompilerParams(vmem_limit_bytes=4 * 2**20),
+    )(owner_steps, place, *come)
+    whole = lax.all_to_all(send, ("x", "y"), 0, 0, tiled=True)
+    whole = whole.reshape(PLANES, STEPS, 8, 4, LANES)
+    up = [(i, i + 1) for i in range(slabs - 1)]
+    down = [(j, i) for i, j in up]
+    low = lax.ppermute(whole[PLANES - HALO :], "gz", up)
+    high = lax.ppermute(whole[:HALO], "gz", down)
+    return low, whole, high
 
 
 def local(base_store, perturbations, owner_steps, w_in, b_in, w_mid, b_mid, w_out):
@@ -256,18 +256,18 @@
     down = [(j, i) for i, j in up]
     low = lax.ppermute(state[PLANES - HALO :], "gz", up)
     high = lax.ppermute(state[:HALO], "gz", down)
-    come = spread_base(base_store, owner_steps, slabs)
-    place = jnp.stack([lax.axis_index("y"), slab, jnp.int32(slabs)]).astype(jnp.int32)
+    place = jnp.stack([slab, jnp.int32(slabs), lax.axis_index("h")]).astype(jnp.int32)
+    come = spread_base(base_store, owner_steps, place, slabs)
     vmem = pl.BlockSpec(memory_space=pltpu.VMEM)
     f32, bf16 = jnp.float32, jnp.bfloat16
     new = pl.pallas_call(
         kernel,
         out_shape=jax.ShapeDtypeStruct((PLANES, 8, PLANE), f32),
-        in_specs=[pl.BlockSpec(memory_space=pltpu.SMEM)] + [vmem] * 13,
+        in_specs=[pl.BlockSpec(memory_space=pltpu.SMEM)] + [vmem] * 12,
         out_specs=vmem,
         scratch_shapes=[
             pltpu.VMEM((EXT, 8, PLANE), f32),
-            pltpu.VMEM((4 * BLOCK, 8, PLANE), f32),
+            pltpu.VMEM((EXT, 8, PLANE), f32),
             pltpu.VMEM((EXT, PROWS, PLANE), bf16),
             pltpu.VMEM((EXT, BROWS, PLANE), bf16),
             pltpu.VMEM((EXT, 8, PLANE), f32),
@@ -276,7 +276,7 @@
             pltpu.VMEM((3 * UNITS, PLANE), bf16),
             pltpu.VMEM((2 * UNITS, PLANE), bf16),
         ],
-        compiler_params=pltpu.CompilerParams(vmem_limit_bytes=40 * 2**20),
+        compiler_params=pltpu.CompilerParams(vmem_limit_bytes=24 * 2**20),
     )(place, state, low, high, *come, *weights_of(w_in, w_mid, w_out), b_in[:, None], b_mid[:, None])
     return jnp.transpose(new, (1, 0, 2)).reshape(perturbations.shape)
 

time: 118 us -> 101 us (0.86)
  waiting for transfers between devices: 25.6 us -> 17.7 us
  between operations: 6.29 us -> 0.27 us
  starting transfers between devices: 41.3 us -> 38 us
  Pallas kernels: 34.7 us -> 36.8 us
  local copies, waits for them, and re-layouts: 8.37 us -> 7.14 us
    ppermute x16 -> x5, starting transfers between devices: 35.7 us -> 17.2 us  [the longest x3 8.61 us: spread_base(): lax.ppermute(mine, 'h', [(i, (i + k) % 4) for i in range(4)])]
    ppermute x16 -> x5, waiting for transfers between devices: 25.6 us -> 7.65 us  [the longest x1 4.4 us: spread_base(): high = lax.ppermute(whole[:HALO], 'gz', down)]
    all_to_all x0 -> x2, starting transfers between devices: none -> 14.4 us  [the longest x1 7.58 us: spread_base(): come = lax.all_to_all(tiles, ('x', 'y'), 0, 0, tiled=True)]
    all_to_all x0 -> x2, waiting for transfers between devices: none -> 10 us  [the longest x1 10 us: spread_base(): whole = lax.all_to_all(send, ('x', 'y'), 0, 0, tiled=True)]
    pallas_call x0 -> x2, Pallas kernels: none -> 2.05 us  [the longest x1 1.51 us: spread_base(): pl.pallas_call(take_copies, out_shape=jax.ShapeDtypeStruct((PLANES, STEPS...]
    unnamed x25, local copies, waits for them, and re-layouts: 4.57 us -> 3.1 us
    slice x2 -> x1, local copies, waits for them, and re-layouts: 1.3 us -> 0.04 us  [spread_base(): high = lax.ppermute(whole[:HALO], 'gz', down)]
  transfers between devices with their start and end apart: 18 -> 9, of which waited for: 8 -> 5; matrix products, arithmetic and copies ran while one was open for 3% -> 3% of each run, Pallas kernels for 0% -> 2%
where the time goes in v3:
time: 101 us; the launch traced here: 100 us
  starting transfers between devices  38 us (38%)
  Pallas kernels  36.8 us (36%)
  waiting for transfers between devices  17.7 us (18%)
  local copies, waits for them, and re-layouts  7.14 us (7%)
    pallas_call x1, Pallas kernels, local(): pl.pallas_call(kernel, out_shape=jax.ShapeDtypeStruct((PLANES, 8, PLANE),...  34.8 us
    all_to_all x1, waiting for transfers between devices, spread_base(): whole = lax.all_to_all(send, ('x', 'y'), 0, 0, tiled=True)  10 us
    ppermute x3, starting transfers between devices, spread_base(): lax.ppermute(mine, 'h', [(i, (i + k) % 4) for i in range(4)])  8.61 us
    all_to_all x1, starting transfers between devices, spread_base(): come = lax.all_to_all(tiles, ('x', 'y'), 0, 0, tiled=True)  7.58 us
    all_to_all x1, starting transfers between devices, spread_base(): whole = lax.all_to_all(send, ('x', 'y'), 0, 0, tiled=True)  6.8 us
    ppermute x1, starting transfers between devices, spread_base(): low = lax.ppermute(whole[PLANES - HALO:], 'gz', up)  6.52 us
    ppermute x1, waiting for transfers between devices, spread_base(): high = lax.ppermute(whole[:HALO], 'gz', down)  4.4 us
    ppermute x1, starting transfers between devices, local(): low = lax.ppermute(state[PLANES - HALO:], 'gz', up)  3.44 us
  transfers between devices with their start and end apart: 9, of which 5 were waited for; matrix products, arithmetic and copies ran while one was open for 3% of the time, Pallas kernels for 2%

profile of v3, /device:TPU:1, one launch (start us, length us, event | category | flops | bytes accessed | tf_op | source)
XLA Modules:
  0.0 100.5 jit_solution(17296014716191856375)
XLA Ops:
  0.0 1.0 copy.25
  1.0 0.9 copy.15
  1.9 7.6 %all-to-all-start = ((f32[16,4,8,128]{3,2,1,0:T(8,128)}), f32[16,4,8,128]{3,2,1,0:T(8,128)S(1)}, u32[]{:S(2)}, u32[]{:S(2)}) async-start(f32[16,4,8,128]{3,2,1,0:T(8,128)} %bitcast.7), calls=%async_computation | async-start | bytes 524288 | tf_op jit(solution)/shard_map/all_to_all | solution.py:224
  9.5 0.3 copy.27
  9.8 0.7 fusion.2
  10.5 3.0 %collective-permute-start.1 = (f32[6,8,1024]{2,1,0:T(8,128)}, f32[6,8,1024]{2,1,0:T(8,128)S(1)}, u32[]{:S(2)}, u32[]{:S(2)}) collective-permute-start(f32[6,8,1024]{2,1,0:T(8,128)} %get-tuple-element.7), channel_id=1, source_target_pairs={{1,0},{2,1},{3,2},{5,4},{6,5},{7,6},{9,8},{10,9},{11,10},{13,12},{... | collective-permute-start | bytes 589832 | tf_op jit(solution)/shard_map/ppermute | solution.py:258
  13.5 3.4 %collective-permute-start = (f32[6,8,1024]{2,1,0:T(8,128)S(1)}, f32[6,8,1024]{2,1,0:T(8,128)S(1)}, u32[]{:S(2)}, u32[]{:S(2)}) collective-permute-start(f32[6,8,1024]{2,1,0:T(8,128)S(1)} %get-tuple-element.8), channel_id=1, source_target_pairs={{0,1},{1,2},{2,3},{4,5},{5,6},{6,7},{8,9},{9,10},{10,11},{12,13},{... | collective-permute-start | bytes 589832 | tf_op jit(solution)/shard_map/ppermute | solution.py:257
  17.0 0.1 copy.16
  17.3 0.1 copy.17
  17.6 0.6 copy-done
  18.1 0.5 shard_map.82.c0
  18.7 5.4 %collective-permute-start.4 = (f32[3,4,8,128]{3,2,1,0:T(8,128)S(1)}, f32[3,4,8,128]{3,2,1,0:T(8,128)S(1)}, u32[]{:S(2)}, u32[]{:S(2)}) collective-permute-start(f32[3,4,8,128]{3,2,1,0:T(8,128)S(1)} %shard_map.82.c0), channel_id=1, source_target_pairs={{0,192},{64,0},{128,64},{192,128},{1,193},{65,1},{129,65},{193,129... | collective-permute-start | bytes 147464 | tf_op jit(solution)/shard_map/ppermute | solution.py:233
  24.0 1.0 %collective-permute-start.3 = (f32[3,4,8,128]{3,2,1,0:T(8,128)S(1)}, f32[3,4,8,128]{3,2,1,0:T(8,128)S(1)}, u32[]{:S(2)}, u32[]{:S(2)}) collective-permute-start(f32[3,4,8,128]{3,2,1,0:T(8,128)S(1)} %shard_map.82.c0), channel_id=1, source_target_pairs={{0,128},{64,192},{128,0},{192,64},{1,129},{65,193},{129,1},{193,65... | collective-permute-start | bytes 147464 | tf_op jit(solution)/shard_map/ppermute | solution.py:233
  25.0 2.2 %collective-permute-start.2 = (f32[3,4,8,128]{3,2,1,0:T(8,128)S(1)}, f32[3,4,8,128]{3,2,1,0:T(8,128)S(1)}, u32[]{:S(2)}, u32[]{:S(2)}) collective-permute-start(f32[3,4,8,128]{3,2,1,0:T(8,128)S(1)} %shard_map.82.c0), channel_id=1, source_target_pairs={{0,64},{64,128},{128,192},{192,0},{1,65},{65,129},{129,193},{193,1... | collective-permute-start | bytes 147464 | tf_op jit(solution)/shard_map/ppermute | solution.py:233
  27.5 0.7 copy-done.5
  28.2 0.7 copy-done.6
  29.0 1.9 %collective-permute-done.3.c2 = f32[3,4,8,128]{3,2,1,0:T(8,128)S(1)} collective-permute-done((f32[3,4,8,128]{3,2,1,0:T(8,128)S(1)}, f32[3,4,8,128]{3,2,1,0:T(8,128)S(1)}, u32[]{:S(2)}, u32[]{:S(2)}) %collective-permute-start.3) | collective-permute-done | bytes 49184 | tf_op jit(solution)/shard_map/ppermute | solution.py:233
  30.9 0.2 collective-permute-done.2.c1
  31.1 1.5 %shard_map.83 = f32[16,3,4,8,128]{4,3,2,1,0:T(8,128)} custom-call(s32[3]{0:T(128)S(1)} %copy-done, s32[3]{0:T(128)S(1)} %pad_add_fusion.place, f32[3,4,8,128]{3,2,1,0:T(8,128)S(1)} %shard_map.82.c0, f32[3,4,8,128]{3,2,1,0:T(8,128)S(1)} %collective-permute-done.2.c1, f32[3,4,8,128]{3,2,1,0:T(8,128)S(1)} %collective-permute-done.3.c2, ...), custom_call_target="tpu_custom_call" | custom-call | tf_op jit(solution)/shard_map/pallas_call | solution.py:235
  32.6 6.8 %all-to-all-start.1 = ((f32[16,3,4,8,128]{4,3,2,1,0:T(8,128)}), f32[16,3,4,8,128]{4,3,2,1,0:T(8,128)S(1)}, u32[]{:S(2)}, u32[]{:S(2)}) async-start(f32[16,3,4,8,128]{4,3,2,1,0:T(8,128)} %shard_map.83), calls=%async_computation.1 | async-start | bytes 1572864 | tf_op jit(solution)/shard_map/all_to_all | solution.py:242
  39.5 0.2 broadcast_multiply_fusion.1
  39.7 0.1 mul.56
  39.8 0.1 copy.18.wp
  39.9 10.0 %all-to-all-done.1 = f32[16,3,4,8,128]{4,3,2,1,0:T(8,128)S(1)} async-done(((f32[16,3,4,8,128]{4,3,2,1,0:T(8,128)}), f32[16,3,4,8,128]{4,3,2,1,0:T(8,128)S(1)}, u32[]{:S(2)}, u32[]{:S(2)}) %all-to-all-start.1) | async-done | bytes 786464 | tf_op jit(solution)/shard_map/all_to_all | solution.py:242
  50.0 6.5 %collective-permute-start.5 = (f32[6,3,8,4,128]{4,3,2,1,0:T(4,128)S(1)}, f32[6,3,8,4,128]{4,3,2,1,0:T(4,128)S(1)}, u32[]{:S(2)}, u32[]{:S(2)}) collective-permute-start(f32[6,3,8,4,128]{4,3,2,1,0:T(4,128)S(1)} %bitcast.37), channel_id=1, source_target_pairs={{0,1},{1,2},{2,3},{4,5},{5,6},{6,7},{8,9},{9,10},{10,11},{12,13},{... | collective-permute-start | bytes 884744 | tf_op jit(solution)/shard_map/ppermute | solution.py:246
  56.5 2.1 %collective-permute-start.6 = (f32[6,3,8,4,128]{4,3,2,1,0:T(4,128)S(1)}, f32[6,3,8,4,128]{4,3,2,1,0:T(4,128)S(1)}, u32[]{:S(2)}, u32[]{:S(2)}) collective-permute-start(f32[6,3,8,4,128]{4,3,2,1,0:T(4,128)S(1)} %bitcast.36), channel_id=1, source_target_pairs={{1,0},{2,1},{3,2},{5,4},{6,5},{7,6},{9,8},{10,9},{11,10},{13,12},{... | collective-permute-start | bytes 884744 | tf_op jit(solution)/shard_map/ppermute | solution.py:247
  58.7 0.1 broadcast_multiply_fusion
  58.8 0.2 mul.60.wm
  59.0 1.2 %collective-permute-done.5.base_low = f32[6,3,8,4,128]{4,3,2,1,0:T(4,128)S(1)} collective-permute-done((f32[6,3,8,4,128]{4,3,2,1,0:T(4,128)S(1)}, f32[6,3,8,4,128]{4,3,2,1,0:T(4,128)S(1)}, u32[]{:S(2)}, u32[]{:S(2)}) %collective-permute-start.5) | collective-permute-done | bytes 294944 | tf_op jit(solution)/shard_map/ppermute | solution.py:246
  60.2 4.4 %collective-permute-done.6.base_high = f32[6,3,8,4,128]{4,3,2,1,0:T(4,128)S(1)} collective-permute-done((f32[6,3,8,4,128]{4,3,2,1,0:T(4,128)S(1)}, f32[6,3,8,4,128]{4,3,2,1,0:T(4,128)S(1)}, u32[]{:S(2)}, u32[]{:S(2)}) %collective-permute-start.6) | collective-permute-done | bytes 294944 | tf_op jit(solution)/shard_map/ppermute | solution.py:247
  64.6 34.8 %shard_map.84 = f32[16,8,1024]{2,1,0:T(8,128)S(1)} custom-call(s32[3]{0:T(128)S(1)} %pad_add_fusion.place, f32[16,8,1024]{2,1,0:T(8,128)S(1)} %bitcast.32, f32[6,8,1024]{2,1,0:T(8,128)S(1)} %collective-permute-done.low, f32[6,8,1024]{2,1,0:T(8,128)S(1)} %collective-permute-done.1.high, f32[6,3,8,4,128]{4,3,2,1,0:T(4,128)S(1)} %collective-permute-done.5.base_low, ...), custom_call_target="tpu_custom_call" | custom-call | tf_op jit(solution)/shard_map/pallas_call | solution.py:263
  99.4 1.1 %copy.24 = f32[8,16,1024]{2,1,0:T(8,128)} copy(f32[8,16,1024]{2,0,1:T(8,128)S(1)} %bitcast.33) | data formatting | bytes 1048576 | tf_op jit(solution)/shard_map/reshape | solution.py:281
  (41 shorter events, 0.9 us)
Async XLA Ops:
  1.0 8.5 %copy-start.1 = (f32[2,4,16,1024]{3,2,1,0:T(8,128)S(1)}, f32[2,4,16,1024]{3,2,1,0:T(8,128)}, u32[]{:S(2)}) copy-start(f32[2,4,16,1024]{3,2,1,0:T(8,128)} %param.9) | copy-start | bytes 1572868
  1.9 15.7 %all-to-all-start = ((f32[16,4,8,128]{3,2,1,0:T(8,128)}), f32[16,4,8,128]{3,2,1,0:T(8,128)S(1)}, u32[]{:S(2)}, u32[]{:S(2)}) async-start(f32[16,4,8,128]{3,2,1,0:T(8,128)} %bitcast.7), calls=%async_computation | async-start | bytes 524288 | tf_op jit(solution)/shard_map/all_to_all | solution.py:224
  9.8 7.2 %copy-start.2 = (bf16[64,108]{1,0:T(8,128)(2,1)S(1)}, bf16[64,108]{1,0:T(8,128)(2,1)}, u32[]{:S(2)}) copy-start(bf16[64,108]{1,0:T(8,128)(2,1)} %param.11) | copy-start | bytes 41476
  10.5 6.4 %copy-start.4 = (bf16[6,64]{1,0:T(8,128)(2,1)S(1)}, bf16[6,64]{1,0:T(8,128)(2,1)}, u32[]{:S(2)}) copy-start(bf16[6,64]{1,0:T(8,128)(2,1)} %param.15) | copy-start | bytes 2308
  10.5 48.5 %collective-permute-start.1 = (f32[6,8,1024]{2,1,0:T(8,128)}, f32[6,8,1024]{2,1,0:T(8,128)S(1)}, u32[]{:S(2)}, u32[]{:S(2)}) collective-permute-start(f32[6,8,1024]{2,1,0:T(8,128)} %get-tuple-element.7), channel_id=1, source_target_pairs={{1,0},{2,1},{3,2},{5,4},{6,5},{7,6},{9,8},{10,9},{11,10},{13,12},{... | collective-permute-start | bytes 589832 | tf_op jit(solution)/shard_map/ppermute | solution.py:258
  13.5 45.5 %collective-permute-start = (f32[6,8,1024]{2,1,0:T(8,128)S(1)}, f32[6,8,1024]{2,1,0:T(8,128)S(1)}, u32[]{:S(2)}, u32[]{:S(2)}) collective-permute-start(f32[6,8,1024]{2,1,0:T(8,128)S(1)} %get-tuple-element.8), channel_id=1, source_target_pairs={{0,1},{1,2},{2,3},{4,5},{5,6},{6,7},{8,9},{9,10},{10,11},{12,13},{... | collective-permute-start | bytes 589832 | tf_op jit(solution)/shard_map/ppermute | solution.py:257
  17.5 0.7 copy-start
  18.7 10.3 %collective-permute-start.4 = (f32[3,4,8,128]{3,2,1,0:T(8,128)S(1)}, f32[3,4,8,128]{3,2,1,0:T(8,128)S(1)}, u32[]{:S(2)}, u32[]{:S(2)}) collective-permute-start(f32[3,4,8,128]{3,2,1,0:T(8,128)S(1)} %shard_map.82.c0), channel_id=1, source_target_pairs={{0,192},{64,0},{128,64},{192,128},{1,193},{65,1},{129,65},{193,129... | collective-permute-start | bytes 147464 | tf_op jit(solution)/shard_map/ppermute | solution.py:233
  24.0 6.8 %collective-permute-start.3 = (f32[3,4,8,128]{3,2,1,0:T(8,128)S(1)}, f32[3,4,8,128]{3,2,1,0:T(8,128)S(1)}, u32[]{:S(2)}, u32[]{:S(2)}) collective-permute-start(f32[3,4,8,128]{3,2,1,0:T(8,128)S(1)} %shard_map.82.c0), channel_id=1, source_target_pairs={{0,128},{64,192},{128,0},{192,64},{1,129},{65,193},{129,1},{193,65... | collective-permute-start | bytes 147464 | tf_op jit(solution)/shard_map/ppermute | solution.py:233
  25.0 6.0 %collective-permute-start.2 = (f32[3,4,8,128]{3,2,1,0:T(8,128)S(1)}, f32[3,4,8,128]{3,2,1,0:T(8,128)S(1)}, u32[]{:S(2)}, u32[]{:S(2)}) collective-permute-start(f32[3,4,8,128]{3,2,1,0:T(8,128)S(1)} %shard_map.82.c0), channel_id=1, source_target_pairs={{0,64},{64,128},{128,192},{192,0},{1,65},{65,129},{129,193},{193,1... | collective-permute-start | bytes 147464 | tf_op jit(solution)/shard_map/ppermute | solution.py:233
  27.5 0.7 copy-start.5
  28.2 0.7 copy-start.6
  32.6 17.4 %all-to-all-start.1 = ((f32[16,3,4,8,128]{4,3,2,1,0:T(8,128)}), f32[16,3,4,8,128]{4,3,2,1,0:T(8,128)S(1)}, u32[]{:S(2)}, u32[]{:S(2)}) async-start(f32[16,3,4,8,128]{4,3,2,1,0:T(8,128)} %shard_map.83), calls=%async_computation.1 | async-start | bytes 1572864 | tf_op jit(solution)/shard_map/all_to_all | solution.py:242
  50.0 8.7 %copy-start.3 = (bf16[64,64]{1,0:T(8,128)(2,1)S(1)}, bf16[64,64]{1,0:T(8,128)(2,1)}, u32[]{:S(2)}) copy-start(bf16[64,64]{1,0:T(8,128)(2,1)} %param.13) | copy-start | bytes 24580
  50.0 10.2 %collective-permute-start.5 = (f32[6,3,8,4,128]{4,3,2,1,0:T(4,128)S(1)}, f32[6,3,8,4,128]{4,3,2,1,0:T(4,128)S(1)}, u32[]{:S(2)}, u32[]{:S(2)}) collective-permute-start(f32[6,3,8,4,128]{4,3,2,1,0:T(4,128)S(1)} %bitcast.37), channel_id=1, source_target_pairs={{0,1},{1,2},{2,3},{4,5},{5,6},{6,7},{8,9},{9,10},{10,11},{12,13},{... | collective-permute-start | bytes 884744 | tf_op jit(solution)/shard_map/ppermute | solution.py:246
  56.5 8.0 %collective-permute-start.6 = (f32[6,3,8,4,128]{4,3,2,1,0:T(4,128)S(1)}, f32[6,3,8,4,128]{4,3,2,1,0:T(4,128)S(1)}, u32[]{:S(2)}, u32[]{:S(2)}) collective-permute-start(f32[6,3,8,4,128]{4,3,2,1,0:T(4,128)S(1)} %bitcast.36), channel_id=1, source_target_pairs={{1,0},{2,1},{3,2},{5,4},{6,5},{7,6},{9,8},{10,9},{11,10},{13,12},{... | collective-permute-start | bytes 884744 | tf_op jit(solution)/shard_map/ppermute | solution.py:247

commit v4 on v3

--- a/solution.py
+++ b/solution.py
@@ -94,11 +94,14 @@
         mid_in[2 * UNITS :, cells] = (slope * lin[UNITS:]).astype(bf16)
 
     def layer_two(cells):
-        lin = jnp.dot(wm[...], mid_in[:, cells], preferred_element_type=f32)
-        second = jnp.tanh(lin[:UNITS] + bias[1])
+        def product(k):
+            rows = slice(k * UNITS, (k + 1) * UNITS)
+            return jnp.dot(wm[...], mid_in[rows, cells], preferred_element_type=f32)
+
+        second = jnp.tanh(product(0) + bias[1])
         slope = 1.0 - second * second
-        out_in[0:UNITS, cells] = (slope * lin[UNITS : 2 * UNITS]).astype(bf16)
-        out_in[UNITS:, cells] = (slope * lin[2 * UNITS :]).astype(bf16)
+        out_in[0:UNITS, cells] = (slope * product(1)).astype(bf16)
+        out_in[UNITS:, cells] = (slope * product(2)).astype(bf16)
 
     def layer_three(e, cells, keep):
         stress = jnp.dot(wo[...], out_in[:, cells], preferred_element_type=f32)
@@ -143,22 +146,24 @@
 
         def body(i, ahead, one, two, three, after):
             gx, gy = [], []
-            for n in range(PLANE // CHUNK):
-                cells = slice(n * CHUNK, (n + 1) * CHUNK)
-                if three:
+            cuts = [slice(n * CHUNK, (n + 1) * CHUNK) for n in range(PLANE // CHUNK)]
+            if ahead:
+                patches(i)
+            if three:
+                for cells in cuts:
                     g = layer_three(i - 4, cells, inside(i - 4))
                     gz[i - 4, :, cells] = g[2]
                     for half in range(CHUNK // LANES):
                         gx.append(g[0][:, half * LANES : (half + 1) * LANES])
                         gy.append(g[1][:, half * LANES : (half + 1) * LANES])
-                if two:
+            if two:
+                for cells in cuts:
                     layer_two(cells)
-                if one:
+            if one:
+                for cells in cuts:
                     layer_one(i - 2, cells)
             if three:
                 divergence(i - 4, gx, gy)
-            if ahead:
-                patches(i)
             if after:
                 update(i - 6)
 
@@ -173,7 +178,7 @@
         def _(i):
             body(i, True, True, True, True, False)
 
-        @pl.loop(lo + 8, hi)
+        @pl.loop(lo + 8, hi, unroll=2)
         def _(i):
             body(i, True, True, True, True, True)
 
@@ -191,13 +196,18 @@
     wp = wp.reshape(2 * UNITS, 3 * PROWS)
     order = (0, 2, 3, 5, 6, 8, 1, 7, 4, 9, 9, 9)
     wb = jnp.concatenate([split[:, :, i : i + 1] for i in order], axis=2).reshape(UNITS, 3 * BROWS)
-    wm = jnp.eye(3, dtype=bf16)[:, None, :, None] * w_mid[None, :, None, :]
-    wm = wm.reshape(3 * UNITS, 3 * UNITS)
     out_pad = jnp.pad(w_out, ((0, 1), (0, 0)))
     comps = (0, 3, 4, 6, 3, 1, 5, 6, 4, 5, 2, 6)
     rows = jnp.concatenate([out_pad[i : i + 1] for i in comps], axis=0).reshape(3, 1, 4, 1, UNITS)
     wo = (rows * eye[None, :, None, :, None]).reshape(24, 2 * UNITS)
-    return wp, wb, wm, wo
+    return wp, wb, w_mid, wo
+
+
+def regroup(planes, tiles):
+    for field in range(4):
+        for k in range(PLANE // LANES):
+            rows = planes[field, :, k * LANES : (k + 1) * LANES]
+            tiles[:, k // 2, 4 * (k % 2) + field, :] = rows
 
 
 def take_plane(owner, come, mine):
@@ -218,9 +228,13 @@
 def spread_base(base_store, owner_steps, place, slabs):
     f32 = jnp.float32
     smem, vmem = (pl.BlockSpec(memory_space=m) for m in (pltpu.SMEM, pltpu.VMEM))
-    tiles = jnp.transpose(base_store[0], (1, 0, 2)).reshape(PLANES, 4, 8, LANES)
-    tiles = jnp.transpose(tiles, (0, 2, 1, 3))
-    tiles = tiles.reshape(PLANES, 4, 8, LANES)
+    tiles = pl.pallas_call(
+        regroup,
+        out_shape=jax.ShapeDtypeStruct((PLANES, 4, 8, LANES), f32),
+        in_specs=[vmem],
+        out_specs=vmem,
+        compiler_params=pltpu.CompilerParams(vmem_limit_bytes=4 * 2**20),
+    )(base_store[0])
     come = lax.all_to_all(tiles, ("x", "y"), 0, 0, tiled=True)
     mine = pl.pallas_call(
         take_plane,

time: 101 us -> 96.2 us (0.952)
  Pallas kernels: 36.8 us -> 33 us
  local copies, waits for them, and re-layouts: 7.14 us -> 6.05 us
    pallas_call x1, Pallas kernels: 34.8 us -> 30.1 us  [local(): pl.pallas_call(kernel, out_shape=jax.ShapeDtypeStruct((PLANES, 8, PLANE),...]
    ppermute x3, waiting for transfers between devices: 2.07 us -> 3.71 us  [spread_base(): lax.ppermute(mine, 'h', [(i, (i + k) % 4) for i in range(4)])]
    all_to_all x1, waiting for transfers between devices: 10 us -> 8.91 us  [spread_base(): whole = lax.all_to_all(send, ('x', 'y'), 0, 0, tiled=True)]
    unnamed x25 -> x26, local copies, waits for them, and re-layouts: 3.1 us -> 3.05 us
where the time goes in v4:
time: 96.2 us; the launch traced here: 95.7 us
  starting transfers between devices  38 us (40%)
  Pallas kernels  33 us (34%)
  waiting for transfers between devices  18 us (19%)
  local copies, waits for them, and re-layouts  6.05 us (6%)
    pallas_call x1, Pallas kernels, local(): pl.pallas_call(kernel, out_shape=jax.ShapeDtypeStruct((PLANES, 8, PLANE),...  30.1 us
    all_to_all x1, waiting for transfers between devices, spread_base(): whole = lax.all_to_all(send, ('x', 'y'), 0, 0, tiled=True)  8.91 us
    ppermute x3, starting transfers between devices, spread_base(): lax.ppermute(mine, 'h', [(i, (i + k) % 4) for i in range(4)])  8.61 us
    all_to_all x1, starting transfers between devices, spread_base(): come = lax.all_to_all(tiles, ('x', 'y'), 0, 0, tiled=True)  7.58 us
    all_to_all x1, starting transfers between devices, spread_base(): whole = lax.all_to_all(send, ('x', 'y'), 0, 0, tiled=True)  6.77 us
    ppermute x1, starting transfers between devices, spread_base(): low = lax.ppermute(whole[PLANES - HALO:], 'gz', up)  6.52 us
    ppermute x1, waiting for transfers between devices, spread_base(): high = lax.ppermute(whole[:HALO], 'gz', down)  4.4 us
    ppermute x3, waiting for transfers between devices, spread_base(): lax.ppermute(mine, 'h', [(i, (i + k) % 4) for i in range(4)])  3.71 us
  transfers between devices with their start and end apart: 9, of which 5 were waited for; matrix products, arithmetic and copies ran while one was open for 3% of the time, Pallas kernels for 2%

profile of v4, /device:TPU:1, one launch (start us, length us, event | category | flops | bytes accessed | tf_op | source)
XLA Modules:
  0.0 95.7 jit_solution(18082914431045500843)
XLA Ops:
  0.0 0.9 copy-done
  1.0 0.9 shard_map.82
  1.8 7.6 %all-to-all-start = ((f32[16,4,8,128]{3,2,1,0:T(8,128)}), f32[16,4,8,128]{3,2,1,0:T(8,128)S(1)}, u32[]{:S(2)}, u32[]{:S(2)}) async-start(f32[16,4,8,128]{3,2,1,0:T(8,128)} %shard_map.82), calls=%async_computation | async-start | bytes 524288 | tf_op jit(solution)/shard_map/all_to_all | solution.py:238
  9.5 0.3 copy.24
  9.8 0.7 fusion.1
  10.5 3.0 %collective-permute-start.1 = (f32[6,8,1024]{2,1,0:T(8,128)}, f32[6,8,1024]{2,1,0:T(8,128)S(1)}, u32[]{:S(2)}, u32[]{:S(2)}) collective-permute-start(f32[6,8,1024]{2,1,0:T(8,128)} %get-tuple-element.7), channel_id=1, source_target_pairs={{1,0},{2,1},{3,2},{5,4},{6,5},{7,6},{9,8},{10,9},{11,10},{13,12},{... | collective-permute-start | bytes 589832 | tf_op jit(solution)/shard_map/ppermute | solution.py:272
  13.5 3.4 %collective-permute-start = (f32[6,8,1024]{2,1,0:T(8,128)S(1)}, f32[6,8,1024]{2,1,0:T(8,128)S(1)}, u32[]{:S(2)}, u32[]{:S(2)}) collective-permute-start(f32[6,8,1024]{2,1,0:T(8,128)S(1)} %get-tuple-element.8), channel_id=1, source_target_pairs={{0,1},{1,2},{2,3},{4,5},{5,6},{6,7},{8,9},{9,10},{10,11},{12,13},{... | collective-permute-start | bytes 589832 | tf_op jit(solution)/shard_map/ppermute | solution.py:271
  17.0 0.1 copy.14
  17.2 0.1 copy.15
  17.5 0.6 copy-done.2
  18.1 0.5 shard_map.83.c0
  18.6 5.4 %collective-permute-start.4 = (f32[3,4,8,128]{3,2,1,0:T(8,128)S(1)}, f32[3,4,8,128]{3,2,1,0:T(8,128)S(1)}, u32[]{:S(2)}, u32[]{:S(2)}) collective-permute-start(f32[3,4,8,128]{3,2,1,0:T(8,128)S(1)} %shard_map.83.c0), channel_id=1, source_target_pairs={{0,192},{64,0},{128,64},{192,128},{1,193},{65,1},{129,65},{193,129... | collective-permute-start | bytes 147464 | tf_op jit(solution)/shard_map/ppermute | solution.py:247
  24.0 1.0 %collective-permute-start.3 = (f32[3,4,8,128]{3,2,1,0:T(8,128)S(1)}, f32[3,4,8,128]{3,2,1,0:T(8,128)S(1)}, u32[]{:S(2)}, u32[]{:S(2)}) collective-permute-start(f32[3,4,8,128]{3,2,1,0:T(8,128)S(1)} %shard_map.83.c0), channel_id=1, source_target_pairs={{0,128},{64,192},{128,0},{192,64},{1,129},{65,193},{129,1},{193,65... | collective-permute-start | bytes 147464 | tf_op jit(solution)/shard_map/ppermute | solution.py:247
  25.0 2.2 %collective-permute-start.2 = (f32[3,4,8,128]{3,2,1,0:T(8,128)S(1)}, f32[3,4,8,128]{3,2,1,0:T(8,128)S(1)}, u32[]{:S(2)}, u32[]{:S(2)}) collective-permute-start(f32[3,4,8,128]{3,2,1,0:T(8,128)S(1)} %shard_map.83.c0), channel_id=1, source_target_pairs={{0,64},{64,128},{128,192},{192,0},{1,65},{65,129},{129,193},{193,1... | collective-permute-start | bytes 147464 | tf_op jit(solution)/shard_map/ppermute | solution.py:247
  27.3 3.5 %collective-permute-done.3.c2 = f32[3,4,8,128]{3,2,1,0:T(8,128)S(1)} collective-permute-done((f32[3,4,8,128]{3,2,1,0:T(8,128)S(1)}, f32[3,4,8,128]{3,2,1,0:T(8,128)S(1)}, u32[]{:S(2)}, u32[]{:S(2)}) %collective-permute-start.3) | collective-permute-done | bytes 49184 | tf_op jit(solution)/shard_map/ppermute | solution.py:247
  30.8 0.2 collective-permute-done.2.c1
  31.0 1.5 %shard_map.84 = f32[16,3,4,8,128]{4,3,2,1,0:T(8,128)} custom-call(s32[3]{0:T(128)S(1)} %copy-done.2, s32[3]{0:T(128)S(1)} %pad_add_fusion.place, f32[3,4,8,128]{3,2,1,0:T(8,128)S(1)} %shard_map.83.c0, f32[3,4,8,128]{3,2,1,0:T(8,128)S(1)} %collective-permute-done.2.c1, f32[3,4,8,128]{3,2,1,0:T(8,128)S(1)} %collective-permute-done.3.c2, ...), custom_call_target="tpu_custom_call" | custom-call | tf_op jit(solution)/shard_map/pallas_call | solution.py:249
  32.5 6.8 %all-to-all-start.1 = ((f32[16,3,4,8,128]{4,3,2,1,0:T(8,128)}), f32[16,3,4,8,128]{4,3,2,1,0:T(8,128)S(1)}, u32[]{:S(2)}, u32[]{:S(2)}) async-start(f32[16,3,4,8,128]{4,3,2,1,0:T(8,128)} %shard_map.84), calls=%async_computation.1 | async-start | bytes 1572864 | tf_op jit(solution)/shard_map/all_to_all | solution.py:256
  39.4 0.7 copy-done.6
  40.1 0.1 copy.18.b_in
  40.2 0.7 copy-done.7
  40.9 0.1 copy.19.b_mid
  41.0 8.9 %all-to-all-done.1 = f32[16,3,4,8,128]{4,3,2,1,0:T(8,128)S(1)} async-done(((f32[16,3,4,8,128]{4,3,2,1,0:T(8,128)}), f32[16,3,4,8,128]{4,3,2,1,0:T(8,128)S(1)}, u32[]{:S(2)}, u32[]{:S(2)}) %all-to-all-start.1) | async-done | bytes 786464 | tf_op jit(solution)/shard_map/all_to_all | solution.py:256
  49.9 6.5 %collective-permute-start.5 = (f32[6,3,8,4,128]{4,3,2,1,0:T(4,128)S(1)}, f32[6,3,8,4,128]{4,3,2,1,0:T(4,128)S(1)}, u32[]{:S(2)}, u32[]{:S(2)}) collective-permute-start(f32[6,3,8,4,128]{4,3,2,1,0:T(4,128)S(1)} %bitcast.26), channel_id=1, source_target_pairs={{0,1},{1,2},{2,3},{4,5},{5,6},{6,7},{8,9},{9,10},{10,11},{12,13},{... | collective-permute-start | bytes 884744 | tf_op jit(solution)/shard_map/ppermute | solution.py:260
  56.5 2.1 %collective-permute-start.6 = (f32[6,3,8,4,128]{4,3,2,1,0:T(4,128)S(1)}, f32[6,3,8,4,128]{4,3,2,1,0:T(4,128)S(1)}, u32[]{:S(2)}, u32[]{:S(2)}) collective-permute-start(f32[6,3,8,4,128]{4,3,2,1,0:T(4,128)S(1)} %bitcast.25), channel_id=1, source_target_pairs={{1,0},{2,1},{3,2},{5,4},{6,5},{7,6},{9,8},{10,9},{11,10},{13,12},{... | collective-permute-start | bytes 884744 | tf_op jit(solution)/shard_map/ppermute | solution.py:261
  58.7 0.2 broadcast_multiply_fusion
  58.9 0.1 mul.39
  59.0 0.1 copy.16.wp
  59.1 1.0 %collective-permute-done.5.base_low = f32[6,3,8,4,128]{4,3,2,1,0:T(4,128)S(1)} collective-permute-done((f32[6,3,8,4,128]{4,3,2,1,0:T(4,128)S(1)}, f32[6,3,8,4,128]{4,3,2,1,0:T(4,128)S(1)}, u32[]{:S(2)}, u32[]{:S(2)}) %collective-permute-start.5) | collective-permute-done | bytes 294944 | tf_op jit(solution)/shard_map/ppermute | solution.py:260
  60.1 4.4 %collective-permute-done.6.base_high = f32[6,3,8,4,128]{4,3,2,1,0:T(4,128)S(1)} collective-permute-done((f32[6,3,8,4,128]{4,3,2,1,0:T(4,128)S(1)}, f32[6,3,8,4,128]{4,3,2,1,0:T(4,128)S(1)}, u32[]{:S(2)}, u32[]{:S(2)}) %collective-permute-start.6) | collective-permute-done | bytes 294944 | tf_op jit(solution)/shard_map/ppermute | solution.py:261
  64.5 30.1 %shard_map.85 = f32[16,8,1024]{2,1,0:T(8,128)S(1)} custom-call(s32[3]{0:T(128)S(1)} %pad_add_fusion.place, f32[16,8,1024]{2,1,0:T(8,128)S(1)} %bitcast.21, f32[6,8,1024]{2,1,0:T(8,128)S(1)} %collective-permute-done.low, f32[6,8,1024]{2,1,0:T(8,128)S(1)} %collective-permute-done.1.high, f32[6,3,8,4,128]{4,3,2,1,0:T(4,128)S(1)} %collective-permute-done.5.base_low, ...), custom_call_target="tpu_custom_call" | custom-call | tf_op jit(solution)/shard_map/pallas_call | solution.py:277
  94.6 1.1 %copy.22 = f32[8,16,1024]{2,1,0:T(8,128)} copy(f32[8,16,1024]{2,0,1:T(8,128)S(1)} %bitcast.22) | data formatting | bytes 1048576 | tf_op jit(solution)/shard_map/reshape | solution.py:295
  (39 shorter events, 0.7 us)
Async XLA Ops:
  0.0 0.9 copy-start
  1.0 8.5 %copy-start.3 = (f32[2,4,16,1024]{3,2,1,0:T(8,128)S(1)}, f32[2,4,16,1024]{3,2,1,0:T(8,128)}, u32[]{:S(2)}) copy-start(f32[2,4,16,1024]{3,2,1,0:T(8,128)} %param.9) | copy-start | bytes 1572868
  1.8 15.6 %all-to-all-start = ((f32[16,4,8,128]{3,2,1,0:T(8,128)}), f32[16,4,8,128]{3,2,1,0:T(8,128)S(1)}, u32[]{:S(2)}, u32[]{:S(2)}) async-start(f32[16,4,8,128]{3,2,1,0:T(8,128)} %shard_map.82), calls=%async_computation | async-start | bytes 524288 | tf_op jit(solution)/shard_map/all_to_all | solution.py:238
  9.8 7.2 %copy-start.4 = (bf16[64,108]{1,0:T(8,128)(2,1)S(1)}, bf16[64,108]{1,0:T(8,128)(2,1)}, u32[]{:S(2)}) copy-start(bf16[64,108]{1,0:T(8,128)(2,1)} %param.11) | copy-start | bytes 41476
  10.5 6.4 %copy-start.5 = (bf16[6,64]{1,0:T(8,128)(2,1)S(1)}, bf16[6,64]{1,0:T(8,128)(2,1)}, u32[]{:S(2)}) copy-start(bf16[6,64]{1,0:T(8,128)(2,1)} %param.15) | copy-start | bytes 2308
  10.5 48.6 %collective-permute-start.1 = (f32[6,8,1024]{2,1,0:T(8,128)}, f32[6,8,1024]{2,1,0:T(8,128)S(1)}, u32[]{:S(2)}, u32[]{:S(2)}) collective-permute-start(f32[6,8,1024]{2,1,0:T(8,128)} %get-tuple-element.7), channel_id=1, source_target_pairs={{1,0},{2,1},{3,2},{5,4},{6,5},{7,6},{9,8},{10,9},{11,10},{13,12},{... | collective-permute-start | bytes 589832 | tf_op jit(solution)/shard_map/ppermute | solution.py:272
  13.5 45.6 %collective-permute-start = (f32[6,8,1024]{2,1,0:T(8,128)S(1)}, f32[6,8,1024]{2,1,0:T(8,128)S(1)}, u32[]{:S(2)}, u32[]{:S(2)}) collective-permute-start(f32[6,8,1024]{2,1,0:T(8,128)S(1)} %get-tuple-element.8), channel_id=1, source_target_pairs={{0,1},{1,2},{2,3},{4,5},{5,6},{6,7},{8,9},{9,10},{10,11},{12,13},{... | collective-permute-start | bytes 589832 | tf_op jit(solution)/shard_map/ppermute | solution.py:271
  17.4 0.7 copy-start.2
  18.6 8.7 %collective-permute-start.4 = (f32[3,4,8,128]{3,2,1,0:T(8,128)S(1)}, f32[3,4,8,128]{3,2,1,0:T(8,128)S(1)}, u32[]{:S(2)}, u32[]{:S(2)}) collective-permute-start(f32[3,4,8,128]{3,2,1,0:T(8,128)S(1)} %shard_map.83.c0), channel_id=1, source_target_pairs={{0,192},{64,0},{128,64},{192,128},{1,193},{65,1},{129,65},{193,129... | collective-permute-start | bytes 147464 | tf_op jit(solution)/shard_map/ppermute | solution.py:247
  24.0 6.9 %collective-permute-start.3 = (f32[3,4,8,128]{3,2,1,0:T(8,128)S(1)}, f32[3,4,8,128]{3,2,1,0:T(8,128)S(1)}, u32[]{:S(2)}, u32[]{:S(2)}) collective-permute-start(f32[3,4,8,128]{3,2,1,0:T(8,128)S(1)} %shard_map.83.c0), channel_id=1, source_target_pairs={{0,128},{64,192},{128,0},{192,64},{1,129},{65,193},{129,1},{193,65... | collective-permute-start | bytes 147464 | tf_op jit(solution)/shard_map/ppermute | solution.py:247
  25.0 6.0 %collective-permute-start.2 = (f32[3,4,8,128]{3,2,1,0:T(8,128)S(1)}, f32[3,4,8,128]{3,2,1,0:T(8,128)S(1)}, u32[]{:S(2)}, u32[]{:S(2)}) collective-permute-start(f32[3,4,8,128]{3,2,1,0:T(8,128)S(1)} %shard_map.83.c0), channel_id=1, source_target_pairs={{0,64},{64,128},{128,192},{192,0},{1,65},{65,129},{129,193},{193,1... | collective-permute-start | bytes 147464 | tf_op jit(solution)/shard_map/ppermute | solution.py:247
  32.5 17.4 %all-to-all-start.1 = ((f32[16,3,4,8,128]{4,3,2,1,0:T(8,128)}), f32[16,3,4,8,128]{4,3,2,1,0:T(8,128)S(1)}, u32[]{:S(2)}, u32[]{:S(2)}) async-start(f32[16,3,4,8,128]{4,3,2,1,0:T(8,128)} %shard_map.84), calls=%async_computation.1 | async-start | bytes 1572864 | tf_op jit(solution)/shard_map/all_to_all | solution.py:256
  39.4 0.7 copy-start.6
  40.2 0.7 copy-start.7
  49.9 10.2 %collective-permute-start.5 = (f32[6,3,8,4,128]{4,3,2,1,0:T(4,128)S(1)}, f32[6,3,8,4,128]{4,3,2,1,0:T(4,128)S(1)}, u32[]{:S(2)}, u32[]{:S(2)}) collective-permute-start(f32[6,3,8,4,128]{4,3,2,1,0:T(4,128)S(1)} %bitcast.26), channel_id=1, source_target_pairs={{0,1},{1,2},{2,3},{4,5},{5,6},{6,7},{8,9},{9,10},{10,11},{12,13},{... | collective-permute-start | bytes 884744 | tf_op jit(solution)/shard_map/ppermute | solution.py:260
  56.5 8.0 %collective-permute-start.6 = (f32[6,3,8,4,128]{4,3,2,1,0:T(4,128)S(1)}, f32[6,3,8,4,128]{4,3,2,1,0:T(4,128)S(1)}, u32[]{:S(2)}, u32[]{:S(2)}) collective-permute-start(f32[6,3,8,4,128]{4,3,2,1,0:T(4,128)S(1)} %bitcast.25), channel_id=1, source_target_pairs={{1,0},{2,1},{3,2},{5,4},{6,5},{7,6},{9,8},{10,9},{11,10},{13,12},{... | collective-permute-start | bytes 884744 | tf_op jit(solution)/shard_map/ppermute | solution.py:261
  59.0 5.5 %copy-start.1 = (bf16[64,64]{1,0:T(8,128)(2,1)S(1)}, bf16[64,64]{1,0:T(8,128)(2,1)}, u32[]{:S(2)}) copy-start(bf16[64,64]{1,0:T(8,128)(2,1)} %wm.1) | copy-start | bytes 24580

commit v5 on v4

--- a/solution.py
+++ b/solution.py
@@ -124,7 +124,7 @@
             (HALO + PLANES, HALO, base_high),
         ):
 
-            @pl.loop(0, planes)
+            @pl.loop(0, planes, unroll=2)
             def _(z):
                 for k in range(parts):
                     rows = ref[z, step, k]
@@ -167,18 +167,18 @@
             if after:
                 update(i - 6)
 
-        @pl.loop(lo, lo + 3)
+        @pl.loop(lo, lo + 3, unroll=3)
         def _(i):
             body(i, True, False, False, False, False)
 
         body(lo + 3, True, True, False, False, False)
         body(lo + 4, True, True, True, False, False)
 
-        @pl.loop(lo + 5, lo + 8)
+        @pl.loop(lo + 5, lo + 8, unroll=3)
         def _(i):
             body(i, True, True, True, True, False)
 
-        @pl.loop(lo + 8, hi, unroll=2)
+        @pl.loop(lo + 8, hi, unroll=4)
         def _(i):
             body(i, True, True, True, True, True)
 

time: 96.2 us -> 91.8 us (0.954)
  Pallas kernels: 33 us -> 28.7 us
    pallas_call x1, Pallas kernels: 30.1 us -> 25.7 us  [local(): pl.pallas_call(kernel, out_shape=jax.ShapeDtypeStruct((PLANES, 8, PLANE),...]
where the time goes in v5:
time: 91.8 us; the launch traced here: 91.3 us
  starting transfers between devices  37.8 us (41%)
  Pallas kernels  28.7 us (31%)
  waiting for transfers between devices  18.2 us (20%)
  local copies, waits for them, and re-layouts  6.05 us (7%)
    pallas_call x1, Pallas kernels, local(): pl.pallas_call(kernel, out_shape=jax.ShapeDtypeStruct((PLANES, 8, PLANE),...  25.7 us
    all_to_all x1, waiting for transfers between devices, spread_base(): whole = lax.all_to_all(send, ('x', 'y'), 0, 0, tiled=True)  8.91 us
    ppermute x3, starting transfers between devices, spread_base(): lax.ppermute(mine, 'h', [(i, (i + k) % 4) for i in range(4)])  8.61 us
    all_to_all x1, starting transfers between devices, spread_base(): come = lax.all_to_all(tiles, ('x', 'y'), 0, 0, tiled=True)  7.58 us
    all_to_all x1, starting transfers between devices, spread_base(): whole = lax.all_to_all(send, ('x', 'y'), 0, 0, tiled=True)  6.77 us
    ppermute x1, starting transfers between devices, spread_base(): low = lax.ppermute(whole[PLANES - HALO:], 'gz', up)  6.52 us
    ppermute x1, waiting for transfers between devices, spread_base(): high = lax.ppermute(whole[:HALO], 'gz', down)  4.4 us
    ppermute x3, waiting for transfers between devices, spread_base(): lax.ppermute(mine, 'h', [(i, (i + k) % 4) for i in range(4)])  3.71 us
  transfers between devices with their start and end apart: 9, of which 5 were waited for; matrix products, arithmetic and copies ran while one was open for 3% of the time, Pallas kernels for 2%

profile of v5, /device:TPU:1, one launch (start us, length us, event | category | flops | bytes accessed | tf_op | source)
XLA Modules:
  0.0 91.3 jit_solution(3967734678019544971)
XLA Ops:
  0.0 0.9 %copy-done = f32[1,4,16,1024]{3,2,1,0:T(8,128)S(1)} copy-done((f32[1,4,16,1024]{3,2,1,0:T(8,128)S(1)}, f32[1,4,16,1024]{3,2,1,0:T(8,128)}, u32[]{:S(2)}) %copy-start) | copy-done | bytes 262168
  1.0 0.9 shard_map.82
  1.8 7.6 %all-to-all-start = ((f32[16,4,8,128]{3,2,1,0:T(8,128)}), f32[16,4,8,128]{3,2,1,0:T(8,128)S(1)}, u32[]{:S(2)}, u32[]{:S(2)}) async-start(f32[16,4,8,128]{3,2,1,0:T(8,128)} %shard_map.82), calls=%async_computation | async-start | bytes 524288 | tf_op jit(solution)/shard_map/all_to_all | solution.py:238
  9.5 0.3 copy.24
  9.8 0.7 fusion.1
  10.5 3.0 %collective-permute-start.1 = (f32[6,8,1024]{2,1,0:T(8,128)}, f32[6,8,1024]{2,1,0:T(8,128)S(1)}, u32[]{:S(2)}, u32[]{:S(2)}) collective-permute-start(f32[6,8,1024]{2,1,0:T(8,128)} %get-tuple-element.7), channel_id=1, source_target_pairs={{1,0},{2,1},{3,2},{5,4},{6,5},{7,6},{9,8},{10,9},{11,10},{13,12},{... | collective-permute-start | bytes 589832 | tf_op jit(solution)/shard_map/ppermute | solution.py:272
  13.5 3.4 %collective-permute-start = (f32[6,8,1024]{2,1,0:T(8,128)S(1)}, f32[6,8,1024]{2,1,0:T(8,128)S(1)}, u32[]{:S(2)}, u32[]{:S(2)}) collective-permute-start(f32[6,8,1024]{2,1,0:T(8,128)S(1)} %get-tuple-element.8), channel_id=1, source_target_pairs={{0,1},{1,2},{2,3},{4,5},{5,6},{6,7},{8,9},{9,10},{10,11},{12,13},{... | collective-permute-start | bytes 589832 | tf_op jit(solution)/shard_map/ppermute | solution.py:271
  17.0 0.1 copy.14
  17.2 0.1 copy.15
  17.5 0.6 copy-done.2
  18.1 0.5 shard_map.83.c0
  18.6 5.4 %collective-permute-start.4 = (f32[3,4,8,128]{3,2,1,0:T(8,128)S(1)}, f32[3,4,8,128]{3,2,1,0:T(8,128)S(1)}, u32[]{:S(2)}, u32[]{:S(2)}) collective-permute-start(f32[3,4,8,128]{3,2,1,0:T(8,128)S(1)} %shard_map.83.c0), channel_id=1, source_target_pairs={{0,192},{64,0},{128,64},{192,128},{1,193},{65,1},{129,65},{193,129... | collective-permute-start | bytes 147464 | tf_op jit(solution)/shard_map/ppermute | solution.py:247
  24.0 1.0 %collective-permute-start.3 = (f32[3,4,8,128]{3,2,1,0:T(8,128)S(1)}, f32[3,4,8,128]{3,2,1,0:T(8,128)S(1)}, u32[]{:S(2)}, u32[]{:S(2)}) collective-permute-start(f32[3,4,8,128]{3,2,1,0:T(8,128)S(1)} %shard_map.83.c0), channel_id=1, source_target_pairs={{0,128},{64,192},{128,0},{192,64},{1,129},{65,193},{129,1},{193,65... | collective-permute-start | bytes 147464 | tf_op jit(solution)/shard_map/ppermute | solution.py:247
  25.0 2.2 %collective-permute-start.2 = (f32[3,4,8,128]{3,2,1,0:T(8,128)S(1)}, f32[3,4,8,128]{3,2,1,0:T(8,128)S(1)}, u32[]{:S(2)}, u32[]{:S(2)}) collective-permute-start(f32[3,4,8,128]{3,2,1,0:T(8,128)S(1)} %shard_map.83.c0), channel_id=1, source_target_pairs={{0,64},{64,128},{128,192},{192,0},{1,65},{65,129},{129,193},{193,1... | collective-permute-start | bytes 147464 | tf_op jit(solution)/shard_map/ppermute | solution.py:247
  27.3 3.5 %collective-permute-done.3.c2 = f32[3,4,8,128]{3,2,1,0:T(8,128)S(1)} collective-permute-done((f32[3,4,8,128]{3,2,1,0:T(8,128)S(1)}, f32[3,4,8,128]{3,2,1,0:T(8,128)S(1)}, u32[]{:S(2)}, u32[]{:S(2)}) %collective-permute-start.3) | collective-permute-done | bytes 49184 | tf_op jit(solution)/shard_map/ppermute | solution.py:247
  30.8 0.2 collective-permute-done.2.c1
  31.0 1.5 %shard_map.84 = f32[16,3,4,8,128]{4,3,2,1,0:T(8,128)} custom-call(s32[3]{0:T(128)S(1)} %copy-done.2, s32[3]{0:T(128)S(1)} %pad_add_fusion.place, f32[3,4,8,128]{3,2,1,0:T(8,128)S(1)} %shard_map.83.c0, f32[3,4,8,128]{3,2,1,0:T(8,128)S(1)} %collective-permute-done.2.c1, f32[3,4,8,128]{3,2,1,0:T(8,128)S(1)} %collective-permute-done.3.c2, ...), custom_call_target="tpu_custom_call" | custom-call | tf_op jit(solution)/shard_map/pallas_call | solution.py:249
  32.5 6.8 %all-to-all-start.1 = ((f32[16,3,4,8,128]{4,3,2,1,0:T(8,128)}), f32[16,3,4,8,128]{4,3,2,1,0:T(8,128)S(1)}, u32[]{:S(2)}, u32[]{:S(2)}) async-start(f32[16,3,4,8,128]{4,3,2,1,0:T(8,128)} %shard_map.84), calls=%async_computation.1 | async-start | bytes 1572864 | tf_op jit(solution)/shard_map/all_to_all | solution.py:256
  39.4 0.7 copy-done.6
  40.1 0.1 copy.18.b_in
  40.2 0.7 copy-done.7
  40.9 0.1 copy.19.b_mid
  41.0 8.9 %all-to-all-done.1 = f32[16,3,4,8,128]{4,3,2,1,0:T(8,128)S(1)} async-done(((f32[16,3,4,8,128]{4,3,2,1,0:T(8,128)}), f32[16,3,4,8,128]{4,3,2,1,0:T(8,128)S(1)}, u32[]{:S(2)}, u32[]{:S(2)}) %all-to-all-start.1) | async-done | bytes 786464 | tf_op jit(solution)/shard_map/all_to_all | solution.py:256
  49.9 6.5 %collective-permute-start.5 = (f32[6,3,8,4,128]{4,3,2,1,0:T(4,128)S(1)}, f32[6,3,8,4,128]{4,3,2,1,0:T(4,128)S(1)}, u32[]{:S(2)}, u32[]{:S(2)}) collective-permute-start(f32[6,3,8,4,128]{4,3,2,1,0:T(4,128)S(1)} %bitcast.26), channel_id=1, source_target_pairs={{0,1},{1,2},{2,3},{4,5},{5,6},{6,7},{8,9},{9,10},{10,11},{12,13},{... | collective-permute-start | bytes 884744 | tf_op jit(solution)/shard_map/ppermute | solution.py:260
  56.5 1.9 %collective-permute-start.6 = (f32[6,3,8,4,128]{4,3,2,1,0:T(4,128)S(1)}, f32[6,3,8,4,128]{4,3,2,1,0:T(4,128)S(1)}, u32[]{:S(2)}, u32[]{:S(2)}) collective-permute-start(f32[6,3,8,4,128]{4,3,2,1,0:T(4,128)S(1)} %bitcast.25), channel_id=1, source_target_pairs={{1,0},{2,1},{3,2},{5,4},{6,5},{7,6},{9,8},{10,9},{11,10},{13,12},{... | collective-permute-start | bytes 884744 | tf_op jit(solution)/shard_map/ppermute | solution.py:261
  58.5 0.2 broadcast_multiply_fusion
  58.7 0.1 mul.39
  58.8 0.1 copy.16.wp
  58.9 1.2 %collective-permute-done.5.base_low = f32[6,3,8,4,128]{4,3,2,1,0:T(4,128)S(1)} collective-permute-done((f32[6,3,8,4,128]{4,3,2,1,0:T(4,128)S(1)}, f32[6,3,8,4,128]{4,3,2,1,0:T(4,128)S(1)}, u32[]{:S(2)}, u32[]{:S(2)}) %collective-permute-start.5) | collective-permute-done | bytes 294944 | tf_op jit(solution)/shard_map/ppermute | solution.py:260
  60.1 4.4 %collective-permute-done.6.base_high = f32[6,3,8,4,128]{4,3,2,1,0:T(4,128)S(1)} collective-permute-done((f32[6,3,8,4,128]{4,3,2,1,0:T(4,128)S(1)}, f32[6,3,8,4,128]{4,3,2,1,0:T(4,128)S(1)}, u32[]{:S(2)}, u32[]{:S(2)}) %collective-permute-start.6) | collective-permute-done | bytes 294944 | tf_op jit(solution)/shard_map/ppermute | solution.py:261
  64.5 25.7 %shard_map.85 = f32[16,8,1024]{2,1,0:T(8,128)S(1)} custom-call(s32[3]{0:T(128)S(1)} %pad_add_fusion.place, f32[16,8,1024]{2,1,0:T(8,128)S(1)} %bitcast.21, f32[6,8,1024]{2,1,0:T(8,128)S(1)} %collective-permute-done.low, f32[6,8,1024]{2,1,0:T(8,128)S(1)} %collective-permute-done.1.high, f32[6,3,8,4,128]{4,3,2,1,0:T(4,128)S(1)} %collective-permute-done.5.base_low, ...), custom_call_target="tpu_custom_call" | custom-call | tf_op jit(solution)/shard_map/pallas_call | solution.py:277
  90.2 1.1 %copy.22 = f32[8,16,1024]{2,1,0:T(8,128)} copy(f32[8,16,1024]{2,0,1:T(8,128)S(1)} %bitcast.22) | data formatting | bytes 1048576 | tf_op jit(solution)/shard_map/reshape | solution.py:295
  (39 shorter events, 0.7 us)
Async XLA Ops:
  0.0 0.9 %copy-start = (f32[1,4,16,1024]{3,2,1,0:T(8,128)S(1)}, f32[1,4,16,1024]{3,2,1,0:T(8,128)}, u32[]{:S(2)}) copy-start(f32[1,4,16,1024]{3,2,1,0:T(8,128)} %param.8) | copy-start | bytes 786436
  1.0 8.5 %copy-start.3 = (f32[2,4,16,1024]{3,2,1,0:T(8,128)S(1)}, f32[2,4,16,1024]{3,2,1,0:T(8,128)}, u32[]{:S(2)}) copy-start(f32[2,4,16,1024]{3,2,1,0:T(8,128)} %param.9) | copy-start | bytes 1572868
  1.8 15.6 %all-to-all-start = ((f32[16,4,8,128]{3,2,1,0:T(8,128)}), f32[16,4,8,128]{3,2,1,0:T(8,128)S(1)}, u32[]{:S(2)}, u32[]{:S(2)}) async-start(f32[16,4,8,128]{3,2,1,0:T(8,128)} %shard_map.82), calls=%async_computation | async-start | bytes 524288 | tf_op jit(solution)/shard_map/all_to_all | solution.py:238
  9.8 7.2 %copy-start.4 = (bf16[64,108]{1,0:T(8,128)(2,1)S(1)}, bf16[64,108]{1,0:T(8,128)(2,1)}, u32[]{:S(2)}) copy-start(bf16[64,108]{1,0:T(8,128)(2,1)} %param.11) | copy-start | bytes 41476
  10.5 6.4 %copy-start.5 = (bf16[6,64]{1,0:T(8,128)(2,1)S(1)}, bf16[6,64]{1,0:T(8,128)(2,1)}, u32[]{:S(2)}) copy-start(bf16[6,64]{1,0:T(8,128)(2,1)} %param.15) | copy-start | bytes 2308
  10.5 48.4 %collective-permute-start.1 = (f32[6,8,1024]{2,1,0:T(8,128)}, f32[6,8,1024]{2,1,0:T(8,128)S(1)}, u32[]{:S(2)}, u32[]{:S(2)}) collective-permute-start(f32[6,8,1024]{2,1,0:T(8,128)} %get-tuple-element.7), channel_id=1, source_target_pairs={{1,0},{2,1},{3,2},{5,4},{6,5},{7,6},{9,8},{10,9},{11,10},{13,12},{... | collective-permute-start | bytes 589832 | tf_op jit(solution)/shard_map/ppermute | solution.py:272
  13.5 45.5 %collective-permute-start = (f32[6,8,1024]{2,1,0:T(8,128)S(1)}, f32[6,8,1024]{2,1,0:T(8,128)S(1)}, u32[]{:S(2)}, u32[]{:S(2)}) collective-permute-start(f32[6,8,1024]{2,1,0:T(8,128)S(1)} %get-tuple-element.8), channel_id=1, source_target_pairs={{0,1},{1,2},{2,3},{4,5},{5,6},{6,7},{8,9},{9,10},{10,11},{12,13},{... | collective-permute-start | bytes 589832 | tf_op jit(solution)/shard_map/ppermute | solution.py:271
  17.4 0.7 copy-start.2
  18.6 8.7 %collective-permute-start.4 = (f32[3,4,8,128]{3,2,1,0:T(8,128)S(1)}, f32[3,4,8,128]{3,2,1,0:T(8,128)S(1)}, u32[]{:S(2)}, u32[]{:S(2)}) collective-permute-start(f32[3,4,8,128]{3,2,1,0:T(8,128)S(1)} %shard_map.83.c0), channel_id=1, source_target_pairs={{0,192},{64,0},{128,64},{192,128},{1,193},{65,1},{129,65},{193,129... | collective-permute-start | bytes 147464 | tf_op jit(solution)/shard_map/ppermute | solution.py:247
  24.0 6.9 %collective-permute-start.3 = (f32[3,4,8,128]{3,2,1,0:T(8,128)S(1)}, f32[3,4,8,128]{3,2,1,0:T(8,128)S(1)}, u32[]{:S(2)}, u32[]{:S(2)}) collective-permute-start(f32[3,4,8,128]{3,2,1,0:T(8,128)S(1)} %shard_map.83.c0), channel_id=1, source_target_pairs={{0,128},{64,192},{128,0},{192,64},{1,129},{65,193},{129,1},{193,65... | collective-permute-start | bytes 147464 | tf_op jit(solution)/shard_map/ppermute | solution.py:247
  25.0 6.0 %collective-permute-start.2 = (f32[3,4,8,128]{3,2,1,0:T(8,128)S(1)}, f32[3,4,8,128]{3,2,1,0:T(8,128)S(1)}, u32[]{:S(2)}, u32[]{:S(2)}) collective-permute-start(f32[3,4,8,128]{3,2,1,0:T(8,128)S(1)} %shard_map.83.c0), channel_id=1, source_target_pairs={{0,64},{64,128},{128,192},{192,0},{1,65},{65,129},{129,193},{193,1... | collective-permute-start | bytes 147464 | tf_op jit(solution)/shard_map/ppermute | solution.py:247
  32.5 17.4 %all-to-all-start.1 = ((f32[16,3,4,8,128]{4,3,2,1,0:T(8,128)}), f32[16,3,4,8,128]{4,3,2,1,0:T(8,128)S(1)}, u32[]{:S(2)}, u32[]{:S(2)}) async-start(f32[16,3,4,8,128]{4,3,2,1,0:T(8,128)} %shard_map.84), calls=%async_computation.1 | async-start | bytes 1572864 | tf_op jit(solution)/shard_map/all_to_all | solution.py:256
  39.4 0.7 copy-start.6
  40.2 0.7 copy-start.7
  49.9 10.2 %collective-permute-start.5 = (f32[6,3,8,4,128]{4,3,2,1,0:T(4,128)S(1)}, f32[6,3,8,4,128]{4,3,2,1,0:T(4,128)S(1)}, u32[]{:S(2)}, u32[]{:S(2)}) collective-permute-start(f32[6,3,8,4,128]{4,3,2,1,0:T(4,128)S(1)} %bitcast.26), channel_id=1, source_target_pairs={{0,1},{1,2},{2,3},{4,5},{5,6},{6,7},{8,9},{9,10},{10,11},{12,13},{... | collective-permute-start | bytes 884744 | tf_op jit(solution)/shard_map/ppermute | solution.py:260
  56.5 8.0 %collective-permute-start.6 = (f32[6,3,8,4,128]{4,3,2,1,0:T(4,128)S(1)}, f32[6,3,8,4,128]{4,3,2,1,0:T(4,128)S(1)}, u32[]{:S(2)}, u32[]{:S(2)}) collective-permute-start(f32[6,3,8,4,128]{4,3,2,1,0:T(4,128)S(1)} %bitcast.25), channel_id=1, source_target_pairs={{1,0},{2,1},{3,2},{5,4},{6,5},{7,6},{9,8},{10,9},{11,10},{13,12},{... | collective-permute-start | bytes 884744 | tf_op jit(solution)/shard_map/ppermute | solution.py:261
  58.8 5.7 %copy-start.1 = (bf16[64,64]{1,0:T(8,128)(2,1)S(1)}, bf16[64,64]{1,0:T(8,128)(2,1)}, u32[]{:S(2)}) copy-start(bf16[64,64]{1,0:T(8,128)(2,1)} %wm.1) | copy-start | bytes 24580

commit v6 on v5

--- a/solution.py
+++ b/solution.py
@@ -178,7 +178,7 @@
         def _(i):
             body(i, True, True, True, True, False)
 
-        @pl.loop(lo + 8, hi, unroll=4)
+        @pl.loop(lo + 8, hi, unroll=(5, 8, 6)[step])
         def _(i):
             body(i, True, True, True, True, True)
 

time: 91.8 us -> 91.4 us (level)
  no operation moved by 1% of the time
where the time goes in v6:
time: 91.4 us; the launch traced here: 90.9 us
  starting transfers between devices  38 us (42%)
  Pallas kernels  28.3 us (31%)
  waiting for transfers between devices  18 us (20%)
  local copies, waits for them, and re-layouts  6.05 us (7%)
    pallas_call x1, Pallas kernels, local(): pl.pallas_call(kernel, out_shape=jax.ShapeDtypeStruct((PLANES, 8, PLANE),...  25.3 us
    all_to_all x1, waiting for transfers between devices, spread_base(): whole = lax.all_to_all(send, ('x', 'y'), 0, 0, tiled=True)  8.91 us
    ppermute x3, starting transfers between devices, spread_base(): lax.ppermute(mine, 'h', [(i, (i + k) % 4) for i in range(4)])  8.61 us
    all_to_all x1, starting transfers between devices, spread_base(): come = lax.all_to_all(tiles, ('x', 'y'), 0, 0, tiled=True)  7.58 us
    all_to_all x1, starting transfers between devices, spread_base(): whole = lax.all_to_all(send, ('x', 'y'), 0, 0, tiled=True)  6.77 us
    ppermute x1, starting transfers between devices, spread_base(): low = lax.ppermute(whole[PLANES - HALO:], 'gz', up)  6.52 us
    ppermute x1, waiting for transfers between devices, spread_base(): high = lax.ppermute(whole[:HALO], 'gz', down)  4.4 us
    ppermute x3, waiting for transfers between devices, spread_base(): lax.ppermute(mine, 'h', [(i, (i + k) % 4) for i in range(4)])  3.71 us
  transfers between devices with their start and end apart: 9, of which 5 were waited for; matrix products, arithmetic and copies ran while one was open for 3% of the time, Pallas kernels for 2%

profile of v6, /device:TPU:1, one launch (start us, length us, event | category | flops | bytes accessed | tf_op | source)
XLA Modules:
  0.0 90.9 jit_solution(11073316649413413921)
XLA Ops:
  0.0 0.9 %copy-done = f32[1,4,16,1024]{3,2,1,0:T(8,128)S(1)} copy-done((f32[1,4,16,1024]{3,2,1,0:T(8,128)S(1)}, f32[1,4,16,1024]{3,2,1,0:T(8,128)}, u32[]{:S(2)}) %copy-start) | copy-done | bytes 262168
  1.0 0.9 shard_map.82
  1.8 7.6 %all-to-all-start = ((f32[16,4,8,128]{3,2,1,0:T(8,128)}), f32[16,4,8,128]{3,2,1,0:T(8,128)S(1)}, u32[]{:S(2)}, u32[]{:S(2)}) async-start(f32[16,4,8,128]{3,2,1,0:T(8,128)} %shard_map.82), calls=%async_computation | async-start | bytes 524288 | tf_op jit(solution)/shard_map/all_to_all | solution.py:238
  9.5 0.3 copy.24
  9.8 0.7 fusion.1
  10.5 3.0 %collective-permute-start.1 = (f32[6,8,1024]{2,1,0:T(8,128)}, f32[6,8,1024]{2,1,0:T(8,128)S(1)}, u32[]{:S(2)}, u32[]{:S(2)}) collective-permute-start(f32[6,8,1024]{2,1,0:T(8,128)} %get-tuple-element.7), channel_id=1, source_target_pairs={{1,0},{2,1},{3,2},{5,4},{6,5},{7,6},{9,8},{10,9},{11,10},{13,12},{... | collective-permute-start | bytes 589832 | tf_op jit(solution)/shard_map/ppermute | solution.py:272
  13.5 3.4 %collective-permute-start = (f32[6,8,1024]{2,1,0:T(8,128)S(1)}, f32[6,8,1024]{2,1,0:T(8,128)S(1)}, u32[]{:S(2)}, u32[]{:S(2)}) collective-permute-start(f32[6,8,1024]{2,1,0:T(8,128)S(1)} %get-tuple-element.8), channel_id=1, source_target_pairs={{0,1},{1,2},{2,3},{4,5},{5,6},{6,7},{8,9},{9,10},{10,11},{12,13},{... | collective-permute-start | bytes 589832 | tf_op jit(solution)/shard_map/ppermute | solution.py:271
  17.0 0.1 copy.14
  17.2 0.1 copy.15
  17.5 0.6 copy-done.2
  18.1 0.5 shard_map.83.c0
  18.6 5.4 %collective-permute-start.4 = (f32[3,4,8,128]{3,2,1,0:T(8,128)S(1)}, f32[3,4,8,128]{3,2,1,0:T(8,128)S(1)}, u32[]{:S(2)}, u32[]{:S(2)}) collective-permute-start(f32[3,4,8,128]{3,2,1,0:T(8,128)S(1)} %shard_map.83.c0), channel_id=1, source_target_pairs={{0,192},{64,0},{128,64},{192,128},{1,193},{65,1},{129,65},{193,129... | collective-permute-start | bytes 147464 | tf_op jit(solution)/shard_map/ppermute | solution.py:247
  24.0 1.0 %collective-permute-start.3 = (f32[3,4,8,128]{3,2,1,0:T(8,128)S(1)}, f32[3,4,8,128]{3,2,1,0:T(8,128)S(1)}, u32[]{:S(2)}, u32[]{:S(2)}) collective-permute-start(f32[3,4,8,128]{3,2,1,0:T(8,128)S(1)} %shard_map.83.c0), channel_id=1, source_target_pairs={{0,128},{64,192},{128,0},{192,64},{1,129},{65,193},{129,1},{193,65... | collective-permute-start | bytes 147464 | tf_op jit(solution)/shard_map/ppermute | solution.py:247
  25.0 2.2 %collective-permute-start.2 = (f32[3,4,8,128]{3,2,1,0:T(8,128)S(1)}, f32[3,4,8,128]{3,2,1,0:T(8,128)S(1)}, u32[]{:S(2)}, u32[]{:S(2)}) collective-permute-start(f32[3,4,8,128]{3,2,1,0:T(8,128)S(1)} %shard_map.83.c0), channel_id=1, source_target_pairs={{0,64},{64,128},{128,192},{192,0},{1,65},{65,129},{129,193},{193,1... | collective-permute-start | bytes 147464 | tf_op jit(solution)/shard_map/ppermute | solution.py:247
  27.3 3.5 %collective-permute-done.3.c2 = f32[3,4,8,128]{3,2,1,0:T(8,128)S(1)} collective-permute-done((f32[3,4,8,128]{3,2,1,0:T(8,128)S(1)}, f32[3,4,8,128]{3,2,1,0:T(8,128)S(1)}, u32[]{:S(2)}, u32[]{:S(2)}) %collective-permute-start.3) | collective-permute-done | bytes 49184 | tf_op jit(solution)/shard_map/ppermute | solution.py:247
  30.8 0.2 collective-permute-done.2.c1
  31.0 1.5 %shard_map.84 = f32[16,3,4,8,128]{4,3,2,1,0:T(8,128)} custom-call(s32[3]{0:T(128)S(1)} %copy-done.2, s32[3]{0:T(128)S(1)} %pad_add_fusion.place, f32[3,4,8,128]{3,2,1,0:T(8,128)S(1)} %shard_map.83.c0, f32[3,4,8,128]{3,2,1,0:T(8,128)S(1)} %collective-permute-done.2.c1, f32[3,4,8,128]{3,2,1,0:T(8,128)S(1)} %collective-permute-done.3.c2, ...), custom_call_target="tpu_custom_call" | custom-call | tf_op jit(solution)/shard_map/pallas_call | solution.py:249
  32.5 6.8 %all-to-all-start.1 = ((f32[16,3,4,8,128]{4,3,2,1,0:T(8,128)}), f32[16,3,4,8,128]{4,3,2,1,0:T(8,128)S(1)}, u32[]{:S(2)}, u32[]{:S(2)}) async-start(f32[16,3,4,8,128]{4,3,2,1,0:T(8,128)} %shard_map.84), calls=%async_computation.1 | async-start | bytes 1572864 | tf_op jit(solution)/shard_map/all_to_all | solution.py:256
  39.4 0.7 copy-done.6
  40.1 0.1 copy.18.b_in
  40.2 0.7 copy-done.7
  40.9 0.1 copy.19.b_mid
  41.0 8.9 %all-to-all-done.1 = f32[16,3,4,8,128]{4,3,2,1,0:T(8,128)S(1)} async-done(((f32[16,3,4,8,128]{4,3,2,1,0:T(8,128)}), f32[16,3,4,8,128]{4,3,2,1,0:T(8,128)S(1)}, u32[]{:S(2)}, u32[]{:S(2)}) %all-to-all-start.1) | async-done | bytes 786464 | tf_op jit(solution)/shard_map/all_to_all | solution.py:256
  49.9 6.5 %collective-permute-start.5 = (f32[6,3,8,4,128]{4,3,2,1,0:T(4,128)S(1)}, f32[6,3,8,4,128]{4,3,2,1,0:T(4,128)S(1)}, u32[]{:S(2)}, u32[]{:S(2)}) collective-permute-start(f32[6,3,8,4,128]{4,3,2,1,0:T(4,128)S(1)} %bitcast.26), channel_id=1, source_target_pairs={{0,1},{1,2},{2,3},{4,5},{5,6},{6,7},{8,9},{9,10},{10,11},{12,13},{... | collective-permute-start | bytes 884744 | tf_op jit(solution)/shard_map/ppermute | solution.py:260
  56.5 2.1 %collective-permute-start.6 = (f32[6,3,8,4,128]{4,3,2,1,0:T(4,128)S(1)}, f32[6,3,8,4,128]{4,3,2,1,0:T(4,128)S(1)}, u32[]{:S(2)}, u32[]{:S(2)}) collective-permute-start(f32[6,3,8,4,128]{4,3,2,1,0:T(4,128)S(1)} %bitcast.25), channel_id=1, source_target_pairs={{1,0},{2,1},{3,2},{5,4},{6,5},{7,6},{9,8},{10,9},{11,10},{13,12},{... | collective-permute-start | bytes 884744 | tf_op jit(solution)/shard_map/ppermute | solution.py:261
  58.7 0.2 broadcast_multiply_fusion
  58.9 0.1 mul.39
  59.0 0.1 copy.16.wp
  59.1 1.0 %collective-permute-done.5.base_low = f32[6,3,8,4,128]{4,3,2,1,0:T(4,128)S(1)} collective-permute-done((f32[6,3,8,4,128]{4,3,2,1,0:T(4,128)S(1)}, f32[6,3,8,4,128]{4,3,2,1,0:T(4,128)S(1)}, u32[]{:S(2)}, u32[]{:S(2)}) %collective-permute-start.5) | collective-permute-done | bytes 294944 | tf_op jit(solution)/shard_map/ppermute | solution.py:260
  60.1 4.4 %collective-permute-done.6.base_high = f32[6,3,8,4,128]{4,3,2,1,0:T(4,128)S(1)} collective-permute-done((f32[6,3,8,4,128]{4,3,2,1,0:T(4,128)S(1)}, f32[6,3,8,4,128]{4,3,2,1,0:T(4,128)S(1)}, u32[]{:S(2)}, u32[]{:S(2)}) %collective-permute-start.6) | collective-permute-done | bytes 294944 | tf_op jit(solution)/shard_map/ppermute | solution.py:261
  64.5 25.3 %shard_map.85 = f32[16,8,1024]{2,1,0:T(8,128)S(1)} custom-call(s32[3]{0:T(128)S(1)} %pad_add_fusion.place, f32[16,8,1024]{2,1,0:T(8,128)S(1)} %bitcast.21, f32[6,8,1024]{2,1,0:T(8,128)S(1)} %collective-permute-done.low, f32[6,8,1024]{2,1,0:T(8,128)S(1)} %collective-permute-done.1.high, f32[6,3,8,4,128]{4,3,2,1,0:T(4,128)S(1)} %collective-permute-done.5.base_low, ...), custom_call_target="tpu_custom_call" | custom-call | tf_op jit(solution)/shard_map/pallas_call | solution.py:277
  89.8 1.1 %copy.22 = f32[8,16,1024]{2,1,0:T(8,128)} copy(f32[8,16,1024]{2,0,1:T(8,128)S(1)} %bitcast.22) | data formatting | bytes 1048576 | tf_op jit(solution)/shard_map/reshape | solution.py:295
  (39 shorter events, 0.7 us)
Async XLA Ops:
  0.0 0.9 %copy-start = (f32[1,4,16,1024]{3,2,1,0:T(8,128)S(1)}, f32[1,4,16,1024]{3,2,1,0:T(8,128)}, u32[]{:S(2)}) copy-start(f32[1,4,16,1024]{3,2,1,0:T(8,128)} %param.8) | copy-start | bytes 786436
  1.0 8.5 %copy-start.3 = (f32[2,4,16,1024]{3,2,1,0:T(8,128)S(1)}, f32[2,4,16,1024]{3,2,1,0:T(8,128)}, u32[]{:S(2)}) copy-start(f32[2,4,16,1024]{3,2,1,0:T(8,128)} %param.9) | copy-start | bytes 1572868
  1.8 15.6 %all-to-all-start = ((f32[16,4,8,128]{3,2,1,0:T(8,128)}), f32[16,4,8,128]{3,2,1,0:T(8,128)S(1)}, u32[]{:S(2)}, u32[]{:S(2)}) async-start(f32[16,4,8,128]{3,2,1,0:T(8,128)} %shard_map.82), calls=%async_computation | async-start | bytes 524288 | tf_op jit(solution)/shard_map/all_to_all | solution.py:238
  9.8 7.2 %copy-start.4 = (bf16[64,108]{1,0:T(8,128)(2,1)S(1)}, bf16[64,108]{1,0:T(8,128)(2,1)}, u32[]{:S(2)}) copy-start(bf16[64,108]{1,0:T(8,128)(2,1)} %param.11) | copy-start | bytes 41476
  10.5 6.4 %copy-start.5 = (bf16[6,64]{1,0:T(8,128)(2,1)S(1)}, bf16[6,64]{1,0:T(8,128)(2,1)}, u32[]{:S(2)}) copy-start(bf16[6,64]{1,0:T(8,128)(2,1)} %param.15) | copy-start | bytes 2308
  10.5 48.6 %collective-permute-start.1 = (f32[6,8,1024]{2,1,0:T(8,128)}, f32[6,8,1024]{2,1,0:T(8,128)S(1)}, u32[]{:S(2)}, u32[]{:S(2)}) collective-permute-start(f32[6,8,1024]{2,1,0:T(8,128)} %get-tuple-element.7), channel_id=1, source_target_pairs={{1,0},{2,1},{3,2},{5,4},{6,5},{7,6},{9,8},{10,9},{11,10},{13,12},{... | collective-permute-start | bytes 589832 | tf_op jit(solution)/shard_map/ppermute | solution.py:272
  13.5 45.6 %collective-permute-start = (f32[6,8,1024]{2,1,0:T(8,128)S(1)}, f32[6,8,1024]{2,1,0:T(8,128)S(1)}, u32[]{:S(2)}, u32[]{:S(2)}) collective-permute-start(f32[6,8,1024]{2,1,0:T(8,128)S(1)} %get-tuple-element.8), channel_id=1, source_target_pairs={{0,1},{1,2},{2,3},{4,5},{5,6},{6,7},{8,9},{9,10},{10,11},{12,13},{... | collective-permute-start | bytes 589832 | tf_op jit(solution)/shard_map/ppermute | solution.py:271
  17.4 0.7 copy-start.2
  18.6 8.7 %collective-permute-start.4 = (f32[3,4,8,128]{3,2,1,0:T(8,128)S(1)}, f32[3,4,8,128]{3,2,1,0:T(8,128)S(1)}, u32[]{:S(2)}, u32[]{:S(2)}) collective-permute-start(f32[3,4,8,128]{3,2,1,0:T(8,128)S(1)} %shard_map.83.c0), channel_id=1, source_target_pairs={{0,192},{64,0},{128,64},{192,128},{1,193},{65,1},{129,65},{193,129... | collective-permute-start | bytes 147464 | tf_op jit(solution)/shard_map/ppermute | solution.py:247
  24.0 6.9 %collective-permute-start.3 = (f32[3,4,8,128]{3,2,1,0:T(8,128)S(1)}, f32[3,4,8,128]{3,2,1,0:T(8,128)S(1)}, u32[]{:S(2)}, u32[]{:S(2)}) collective-permute-start(f32[3,4,8,128]{3,2,1,0:T(8,128)S(1)} %shard_map.83.c0), channel_id=1, source_target_pairs={{0,128},{64,192},{128,0},{192,64},{1,129},{65,193},{129,1},{193,65... | collective-permute-start | bytes 147464 | tf_op jit(solution)/shard_map/ppermute | solution.py:247
  25.0 6.0 %collective-permute-start.2 = (f32[3,4,8,128]{3,2,1,0:T(8,128)S(1)}, f32[3,4,8,128]{3,2,1,0:T(8,128)S(1)}, u32[]{:S(2)}, u32[]{:S(2)}) collective-permute-start(f32[3,4,8,128]{3,2,1,0:T(8,128)S(1)} %shard_map.83.c0), channel_id=1, source_target_pairs={{0,64},{64,128},{128,192},{192,0},{1,65},{65,129},{129,193},{193,1... | collective-permute-start | bytes 147464 | tf_op jit(solution)/shard_map/ppermute | solution.py:247
  32.5 17.4 %all-to-all-start.1 = ((f32[16,3,4,8,128]{4,3,2,1,0:T(8,128)}), f32[16,3,4,8,128]{4,3,2,1,0:T(8,128)S(1)}, u32[]{:S(2)}, u32[]{:S(2)}) async-start(f32[16,3,4,8,128]{4,3,2,1,0:T(8,128)} %shard_map.84), calls=%async_computation.1 | async-start | bytes 1572864 | tf_op jit(solution)/shard_map/all_to_all | solution.py:256
  39.4 0.7 copy-start.6
  40.2 0.7 copy-start.7
  49.9 10.2 %collective-permute-start.5 = (f32[6,3,8,4,128]{4,3,2,1,0:T(4,128)S(1)}, f32[6,3,8,4,128]{4,3,2,1,0:T(4,128)S(1)}, u32[]{:S(2)}, u32[]{:S(2)}) collective-permute-start(f32[6,3,8,4,128]{4,3,2,1,0:T(4,128)S(1)} %bitcast.26), channel_id=1, source_target_pairs={{0,1},{1,2},{2,3},{4,5},{5,6},{6,7},{8,9},{9,10},{10,11},{12,13},{... | collective-permute-start | bytes 884744 | tf_op jit(solution)/shard_map/ppermute | solution.py:260
  56.5 8.0 %collective-permute-start.6 = (f32[6,3,8,4,128]{4,3,2,1,0:T(4,128)S(1)}, f32[6,3,8,4,128]{4,3,2,1,0:T(4,128)S(1)}, u32[]{:S(2)}, u32[]{:S(2)}) collective-permute-start(f32[6,3,8,4,128]{4,3,2,1,0:T(4,128)S(1)} %bitcast.25), channel_id=1, source_target_pairs={{1,0},{2,1},{3,2},{5,4},{6,5},{7,6},{9,8},{10,9},{11,10},{13,12},{... | collective-permute-start | bytes 884744 | tf_op jit(solution)/shard_map/ppermute | solution.py:261
  59.0 5.5 %copy-start.1 = (bf16[64,64]{1,0:T(8,128)(2,1)S(1)}, bf16[64,64]{1,0:T(8,128)(2,1)}, u32[]{:S(2)}) copy-start(bf16[64,64]{1,0:T(8,128)(2,1)} %wm.1) | copy-start | bytes 24580
